TPU v7x, 128 devices: a whole 4x4x4 slice. The times are simulated.
128 devices in a mesh: wave: 4 (over x), event: 32 (over z, y, core).
Axes of the slice: x: 4, y: 4, z: 4, core: 2. Of those that a mesh axis runs over, the one named last changes fastest.
Arguments:
- latent: bfloat16 [8, 512, 2048], P(None, 'wave', 'event'), may hold values from -6 to 6
- basis: bfloat16 [1048576, 512], P('event', 'wave'), may hold values from -0.29882812 to 0.29882812
- event_bin: int32 [32, 32768], P('event'), may hold values from 0 to 63, never falling along the last dimension, each value on 1 to 2048 neighbouring positions
- length: float32 [512, 2048], P('wave', 'event'), may hold values from 0.01 to 0.08
- amplitude_scale: float32 [512, 2048], P('wave', 'event'), may hold values from 0.3 to 1
- yield_norm: float32 [512, 2048], P('wave', 'event'), may hold values from 0.5 to 2
- bin_coords: float32 [2, 2048], replicated, may hold values from 0 to 1
Outputs:
- grad_latent: float32 [8, 512, 2048], P(None, 'wave', 'event')
Inputs may be any that keep to these rules, and one draw needn't show every extreme that they name: `event_bin`: along each block's events, bin numbers never fall and every one of the block's bins holds at least one event.
All inputs are finite; a program needn't handle non-finite values.
Results may differ from a plain program's by a relative error of at most 0.0024.
Values may be sent and summed in bfloat16 or wider, within the bound.
No kernel may reach another device: no remote copies, remote signals or barrier semaphores. Data moves between devices by JAX's collectives and lax.ppermute only.
A program may use at most 128 MiB of HBM per device.

v0:
```python
import jax
import jax.numpy as jnp
from jax import lax
from jax.sharding import PartitionSpec as P


def gibbs(rows_xy, cols_xy, len_rows, amp_rows, len_cols, amp_cols):
    diff_x = rows_xy[0][:, None] - cols_xy[0][None, :]
    diff_y = rows_xy[1][:, None] - cols_xy[1][None, :]
    dist = diff_x * diff_x + diff_y * diff_y
    left = len_rows[:, :, None]
    right = len_cols[:, None, :]
    spread = left * left + right * right
    return (
        amp_rows[:, :, None]
        * amp_cols[:, None, :]
        * jnp.sqrt(2.0 * (left * right) / spread)
        * jnp.exp(-dist / spread)
    )


def shards(latent, basis, event_bin, length, amplitude_scale, yield_norm, bin_coords):
    position = lax.axis_index("event")
    waves = length.shape[0]
    rows = length.shape[1]
    samples = latent.shape[0]
    total_bins = bin_coords.shape[1]
    len_all, amp_all = (
        lax.all_gather(length, "event", axis=1, tiled=True),
        lax.all_gather(amplitude_scale, "event", axis=1, tiled=True),
    )
    rows_xy = lax.dynamic_slice_in_dim(bin_coords, position * rows, rows, 1)
    group = min(waves, 16)

    def split_waves(values):
        return values.reshape(waves // group, group, values.shape[1])

    def build(pieces):
        len_rows, amp_rows, len_cols, amp_cols = pieces
        return gibbs(rows_xy, bin_coords, len_rows, amp_rows, len_cols, amp_cols).astype(
            jnp.bfloat16
        )

    kern = lax.map(
        build,
        (
            split_waves(length),
            split_waves(amplitude_scale),
            split_waves(len_all),
            split_waves(amp_all),
        ),
    )
    kern = kern.reshape(waves, rows, total_bins)
    columns = kern
    amp_field = jnp.einsum(
        "wrc,swc->swr",
        columns,
        lax.all_gather(latent, "event", axis=2, tiled=True),
        preferred_element_type=jnp.float32,
    ).astype(jnp.bfloat16)
    amp_rows = jnp.transpose(amp_field, (2, 0, 1)).reshape(rows, samples * waves)
    events = basis.shape[0]
    block = min(events, 2048)
    count = events // block
    basis_blocks = basis.reshape(count, block, waves)
    bin_blocks = event_bin.reshape(count, block)
    labels = jnp.arange(rows, dtype=jnp.int32)

    def forward(pieces):
        psi, seg = pieces
        onehot = (seg[:, None] == labels[None, :]).astype(jnp.bfloat16)
        picked = jnp.dot(onehot, amp_rows, preferred_element_type=jnp.float32).reshape(
            block, samples, waves
        )
        return jnp.sum(picked * psi.astype(jnp.float32)[:, None, :], axis=2).T

    partial_fields = lax.map(forward, (basis_blocks, bin_blocks))
    fields = lax.psum(partial_fields, "wave")

    def backward(total, pieces):
        psi, seg, field = pieces
        weight = -2.0 * field / (1.0 + field * field) / samples
        terms = (weight.T[:, :, None] * psi.astype(jnp.float32)[:, None, :]).astype(jnp.bfloat16)
        terms = terms.reshape(block, samples * waves)
        onehot = (seg[:, None] == labels[None, :]).astype(jnp.bfloat16)
        added = lax.dot_general(
            onehot, terms, (((0,), (0,)), ((), ())), preferred_element_type=jnp.float32
        )
        return (total + added, None)

    start_sums = jnp.zeros((rows, samples * waves), jnp.float32)
    sums, unused = lax.scan(backward, start_sums, (basis_blocks, bin_blocks, fields))
    yield_term = 2.0 / samples * amp_field.astype(jnp.float32) * yield_norm[None]
    yield_rows = jnp.transpose(yield_term, (2, 0, 1)).reshape(rows, samples * waves)
    grad_rows = (sums + yield_rows).astype(jnp.bfloat16)
    piece = lax.all_gather(grad_rows, "event", axis=0, tiled=True)
    size = piece.shape[0]
    columns = kern
    pulled = jnp.einsum(
        "wrc,csw->swr",
        columns,
        piece.reshape(size, samples, waves),
        preferred_element_type=jnp.float32,
    )
    return pulled + latent.astype(jnp.float32)


def solution(mesh):
    placed = (
        P(None, "wave", "event"),
        P("event", "wave"),
        P("event", None),
        P("wave", "event"),
        P("wave", "event"),
        P("wave", "event"),
        P(),
    )
    return jax.shard_map(
        shards, mesh=mesh, in_specs=placed, out_specs=P(None, "wave", "event"), check_vma=False
    )
```

profile of v0, /device:TPU:1, one launch (start us, length us, event | category | flops | bytes accessed | tf_op | source)
XLA Modules:
  0.0 612.3 jit_solution(4029658571503979901)
XLA Ops:
  15.7 40.5 %all-gather.7.cloned.1.call-done = f32[128,2048]{0,1:T(8,128)} async-done(((f32[128,64]{0,1:T(8,128)}), f32[128,2048]{0,1:T(8,128)}) %all-gather.7.cloned.1.call-update) | async-done | bytes 1048592 | tf_op jit(solution)/shard_map/all_gather | solution.py:29
  57.8 42.8 %all-gather.5.cloned.1.call-done = f32[128,2048]{0,1:T(8,128)} async-done(((f32[128,64]{0,1:T(8,128)}), f32[128,2048]{0,1:T(8,128)}) %all-gather.5.cloned.1.call-update) | async-done | bytes 1048592 | tf_op jit(solution)/shard_map/all_gather | solution.py:30
  102.2 75.1 %while.32 = (s32[]{:T(128)}, bf16[8,16,64,2048]{3,2,1,0:T(8,128)(2,1)}, f32[8,16,64]{2,1,0:T(8,128)S(1)}, f32[8,16,2048]{2,1,0:T(8,128)S(1)}, f32[8,16,64]{2,1,0...) while((s32[]{:T(128)}, ...), condition=%wide.region_1.2_spmd, body=%wide.region_0.1_spmd.sunk | while | flops 19694592 | bytes 6375533 | solution.py:44
  184.7 15.3 %convert_multiply_fusion = (f32[64,8,128]{0,1,2:T(8,128)S(1)}, bf16[64,8,128]{0,1,2:T(8,128)(2,1)S(1)}) fusion(f32[64,128]{0,1:T(8,128)S(1)} %copy.56, bf16[128,64,2048]{2,1,0:T(8,128)(2,1)} %bitcast.96, bf16[8,128,2048]{2,0,1:T(8,128)(2,1)} %copy.53), kind=kOutput, calls=%fused_computation.39 | convolution fusion | flops 268632064 | bytes 38174720 | tf_op jit(solution)/shard_map/wrc,swc->swr/dot_general | solution.py:55
  200.2 60.7 %while.33 = (s32[]{:T(128)}, f32[16,8,2048]{2,1,0:T(8,128)}, s32[16,2048]{1,0:T(8,128)S(1)}, bf16[64,1024]{1,0:T(8,128)(2,1)S(1)}, bf16[16,2048,128]{2,1,0:T(8,128)(2,1)}, /*index=5*/s32[]{:T(128)}) while((s32[]{:T(128)}, f32[16,8,2048]{2,1,0:T(8,128)}, s32[16,2048]{1,0:T(8,128)S(1)}, bf16[64,1024]{1,0:T(8,128)(2,1)S(1)}, ...), condition=%wide.region_4.5_spmd.clone, body=%wide.region_2.4_spmd.clone.sunk | while | flops 273006592 | bytes 5071437 | solution.py:77
  261.4 42.8 %all-reduce.2.cloned.1.call-done = f32[16,8,2048]{2,1,0:T(8,128)} async-done(((f32[16,8,2048]{2,1,0:T(8,128)}), f32[16,8,2048]{2,1,0:T(8,128)}) %all-reduce.2.cloned.1.call-update) | async-done | bytes 1048592 | tf_op jit(solution)/shard_map/psum | solution.py:78
  304.2 228.4 %while.34 = (s32[]{:T(128)}, f32[64,1024]{1,0:T(8,128)S(1)}, s32[16,2048]{1,0:T(8,128)S(1)}, f32[16,8,2048]{2,1,0:T(8,128)}, bf16[16,2048,128]{2,1,0:T(8,128)(2,1)}, /*index=5*/s32[]{:T(128)}, s32[]{:T(128)}) while((s32[]{:T(128)}, f32[64,1024]{1,0:T(8,128)S(1)}, s32[16,2048]{1,0:T(8,128)S(1)}, f32[16,8,2048]{2,1,0:T(8,128)}, ...), condition=%wide.region_7.8_spmd.clone, body=%wide.region_6.7_spmd.clone.sunk | while | flops 273235968 | bytes 11886691 | solution.py:92
  306.5 8.6 %multiply_convert_fusion.2 = bf16[2048,8,128]{2,1,0:T(8,128)(2,1)} fusion(f32[2048,128]{1,0:T(8,128)S(1)} %bitcast_convert_fusion.5, f32[2048,8]{1,0:T(8,128)S(1)} %copy.81), kind=kLoop, calls=%fused_computation.25.clone.1 | loop fusion | flops 4194304 | bytes 5308416 | tf_op jit(solution)/shard_map/while/body/eval_jaxpr/convert_element_type | solution.py:83
  320.8 8.6 %multiply_convert_fusion.2 = bf16[2048,8,128]{2,1,0:T(8,128)(2,1)} fusion(f32[2048,128]{1,0:T(8,128)S(1)} %bitcast_convert_fusion.5, f32[2048,8]{1,0:T(8,128)S(1)} %copy.81), kind=kLoop, calls=%fused_computation.25.clone.1 | loop fusion | flops 4194304 | bytes 5308416 | tf_op jit(solution)/shard_map/while/body/eval_jaxpr/convert_element_type | solution.py:83
  335.1 8.6 %multiply_convert_fusion.2 = bf16[2048,8,128]{2,1,0:T(8,128)(2,1)} fusion(f32[2048,128]{1,0:T(8,128)S(1)} %bitcast_convert_fusion.5, f32[2048,8]{1,0:T(8,128)S(1)} %copy.81), kind=kLoop, calls=%fused_computation.25.clone.1 | loop fusion | flops 4194304 | bytes 5308416 | tf_op jit(solution)/shard_map/while/body/eval_jaxpr/convert_element_type | solution.py:83
  349.3 8.6 %multiply_convert_fusion.2 = bf16[2048,8,128]{2,1,0:T(8,128)(2,1)} fusion(f32[2048,128]{1,0:T(8,128)S(1)} %bitcast_convert_fusion.5, f32[2048,8]{1,0:T(8,128)S(1)} %copy.81), kind=kLoop, calls=%fused_computation.25.clone.1 | loop fusion | flops 4194304 | bytes 5308416 | tf_op jit(solution)/shard_map/while/body/eval_jaxpr/convert_element_type | solution.py:83
  363.6 8.6 %multiply_convert_fusion.2 = bf16[2048,8,128]{2,1,0:T(8,128)(2,1)} fusion(f32[2048,128]{1,0:T(8,128)S(1)} %bitcast_convert_fusion.5, f32[2048,8]{1,0:T(8,128)S(1)} %copy.81), kind=kLoop, calls=%fused_computation.25.clone.1 | loop fusion | flops 4194304 | bytes 5308416 | tf_op jit(solution)/shard_map/while/body/eval_jaxpr/convert_element_type | solution.py:83
  377.9 8.6 %multiply_convert_fusion.2 = bf16[2048,8,128]{2,1,0:T(8,128)(2,1)} fusion(f32[2048,128]{1,0:T(8,128)S(1)} %bitcast_convert_fusion.5, f32[2048,8]{1,0:T(8,128)S(1)} %copy.81), kind=kLoop, calls=%fused_computation.25.clone.1 | loop fusion | flops 4194304 | bytes 5308416 | tf_op jit(solution)/shard_map/while/body/eval_jaxpr/convert_element_type | solution.py:83
  392.2 8.6 %multiply_convert_fusion.2 = bf16[2048,8,128]{2,1,0:T(8,128)(2,1)} fusion(f32[2048,128]{1,0:T(8,128)S(1)} %bitcast_convert_fusion.5, f32[2048,8]{1,0:T(8,128)S(1)} %copy.81), kind=kLoop, calls=%fused_computation.25.clone.1 | loop fusion | flops 4194304 | bytes 5308416 | tf_op jit(solution)/shard_map/while/body/eval_jaxpr/convert_element_type | solution.py:83
  406.4 8.6 %multiply_convert_fusion.2 = bf16[2048,8,128]{2,1,0:T(8,128)(2,1)} fusion(f32[2048,128]{1,0:T(8,128)S(1)} %bitcast_convert_fusion.5, f32[2048,8]{1,0:T(8,128)S(1)} %copy.81), kind=kLoop, calls=%fused_computation.25.clone.1 | loop fusion | flops 4194304 | bytes 5308416 | tf_op jit(solution)/shard_map/while/body/eval_jaxpr/convert_element_type | solution.py:83
  420.7 8.6 %multiply_convert_fusion.2 = bf16[2048,8,128]{2,1,0:T(8,128)(2,1)} fusion(f32[2048,128]{1,0:T(8,128)S(1)} %bitcast_convert_fusion.5, f32[2048,8]{1,0:T(8,128)S(1)} %copy.81), kind=kLoop, calls=%fused_computation.25.clone.1 | loop fusion | flops 4194304 | bytes 5308416 | tf_op jit(solution)/shard_map/while/body/eval_jaxpr/convert_element_type | solution.py:83
  435.0 8.6 %multiply_convert_fusion.2 = bf16[2048,8,128]{2,1,0:T(8,128)(2,1)} fusion(f32[2048,128]{1,0:T(8,128)S(1)} %bitcast_convert_fusion.5, f32[2048,8]{1,0:T(8,128)S(1)} %copy.81), kind=kLoop, calls=%fused_computation.25.clone.1 | loop fusion | flops 4194304 | bytes 5308416 | tf_op jit(solution)/shard_map/while/body/eval_jaxpr/convert_element_type | solution.py:83
  449.3 8.6 %multiply_convert_fusion.2 = bf16[2048,8,128]{2,1,0:T(8,128)(2,1)} fusion(f32[2048,128]{1,0:T(8,128)S(1)} %bitcast_convert_fusion.5, f32[2048,8]{1,0:T(8,128)S(1)} %copy.81), kind=kLoop, calls=%fused_computation.25.clone.1 | loop fusion | flops 4194304 | bytes 5308416 | tf_op jit(solution)/shard_map/while/body/eval_jaxpr/convert_element_type | solution.py:83
  463.6 8.6 %multiply_convert_fusion.2 = bf16[2048,8,128]{2,1,0:T(8,128)(2,1)} fusion(f32[2048,128]{1,0:T(8,128)S(1)} %bitcast_convert_fusion.5, f32[2048,8]{1,0:T(8,128)S(1)} %copy.81), kind=kLoop, calls=%fused_computation.25.clone.1 | loop fusion | flops 4194304 | bytes 5308416 | tf_op jit(solution)/shard_map/while/body/eval_jaxpr/convert_element_type | solution.py:83
  477.8 8.6 %multiply_convert_fusion.2 = bf16[2048,8,128]{2,1,0:T(8,128)(2,1)} fusion(f32[2048,128]{1,0:T(8,128)S(1)} %bitcast_convert_fusion.5, f32[2048,8]{1,0:T(8,128)S(1)} %copy.81), kind=kLoop, calls=%fused_computation.25.clone.1 | loop fusion | flops 4194304 | bytes 5308416 | tf_op jit(solution)/shard_map/while/body/eval_jaxpr/convert_element_type | solution.py:83
  492.1 8.6 %multiply_convert_fusion.2 = bf16[2048,8,128]{2,1,0:T(8,128)(2,1)} fusion(f32[2048,128]{1,0:T(8,128)S(1)} %bitcast_convert_fusion.5, f32[2048,8]{1,0:T(8,128)S(1)} %copy.81), kind=kLoop, calls=%fused_computation.25.clone.1 | loop fusion | flops 4194304 | bytes 5308416 | tf_op jit(solution)/shard_map/while/body/eval_jaxpr/convert_element_type | solution.py:83
  506.4 8.6 %multiply_convert_fusion.2 = bf16[2048,8,128]{2,1,0:T(8,128)(2,1)} fusion(f32[2048,128]{1,0:T(8,128)S(1)} %bitcast_convert_fusion.5, f32[2048,8]{1,0:T(8,128)S(1)} %copy.81), kind=kLoop, calls=%fused_computation.25.clone.1 | loop fusion | flops 4194304 | bytes 5308416 | tf_op jit(solution)/shard_map/while/body/eval_jaxpr/convert_element_type | solution.py:83
  533.4 49.2 %all-gather.11.cloned.1.call-done = bf16[2048,1024]{1,0:T(8,128)(2,1)} async-done(((bf16[64,1024]{1,0:T(8,128)(2,1)}), bf16[2048,1024]{1,0:T(8,128)(2,1)}) %all-gather.11.cloned.1.call-update) | async-done | bytes 4194320 | tf_op jit(solution)/shard_map/all_gather | solution.py:96
  589.2 15.6 %fusion.19 = f32[128,8,64]{2,1,0:T(8,128)S(1)} fusion(bf16[128,64,2048]{2,1,0:T(8,128)(2,1)} %bitcast.97, bf16[2048,8,128]{0,2,1:T(8,128)(2,1)} %bitcast.99), kind=kOutput, calls=%fused_computation.35 | convolution fusion | flops 268435456 | bytes 38010880 | tf_op jit(solution)/shard_map/wrc,csw->swr/dot_general | solution.py:99
  (276 shorter events, 262.0 us)
Async XLA Ops:
  6.5 49.7 %all-gather.7.cloned.1.call-start = ((), (), s32[]{:S(2)}) async-start(), calls=%async_computation.1 | async-start | bytes 1081344 | tf_op jit(solution)/shard_map/all_gather | solution.py:29
  7.3 93.4 %all-gather.5.cloned.1.call-start = ((), (), s32[]{:S(2)}) async-start(), calls=%async_computation | async-start | bytes 1081344 | tf_op jit(solution)/shard_map/all_gather | solution.py:30
  8.0 169.3 %all-gather.9.cloned.1.call-start = ((), (), s32[]{:S(2)}) async-start(), calls=%async_computation.2 | async-start | bytes 4325376 | tf_op jit(solution)/shard_map/all_gather | solution.py:58
  9.7 294.5 %all-reduce.2.cloned.1.call-start = ((), (), s32[]{:S(2)}) async-start(), calls=%async_computation.3 | async-start | bytes 2097152 | tf_op jit(solution)/shard_map/psum | solution.py:78
  260.9 321.7 %all-gather.11.cloned.1.call-start = ((), (), s32[]{:S(2)}) async-start(), calls=%async_computation.4 | async-start | bytes 4325376 | tf_op jit(solution)/shard_map/all_gather | solution.py:96
  589.2 15.8 %copy-start = (bf16[8,128,64]{1,2,0:T(8,128)(2,1)S(1)}, bf16[8,128,64]{1,2,0:T(8,128)(2,1)}, u32[]{:S(2)}) copy-start(bf16[8,128,64]{1,2,0:T(8,128)(2,1)} %param.13) | copy-start | bytes 393220
Sparse Core Ops, SparseCore 0:
  9.6 46.5 all-gather.6
  58.5 42.0 all-gather.4
  102.9 45.6 all-gather.8
  261.0 43.1 all-reduce.1
  533.5 49.0 all-gather.10
where the time goes:
time: 616 us; the launch traced here: 612 us
  other arithmetic  243 us (39%)
  waiting for transfers between devices  177 us (29%)
  matrix products  112 us (18%)
  local copies, waits for them, and re-layouts  65.6 us (11%)
  between operations  13.3 us (2%)
    convert_element_type x16, other arithmetic, backward(): (weight.T[:, :, None] * psi.astype(jnp.float32)[:, None, :]).astype(jnp.b...  138 us
    dynamic_update_slice x8, other arithmetic, shards(): lax.map(build, (split_waves(length), split_waves(amplitude_scale), split_...  66.3 us
    dot_general x16, matrix products, backward(): lax.dot_general(onehot, terms, (((0,), (0,)), ((), ())), preferred_elemen...  53 us
    all_gather x1, waiting for transfers between devices, shards(): piece = lax.all_gather(grad_rows, 'event', axis=0, tiled=True)  49.2 us
    all_gather x1, waiting for transfers between devices, shards(): lax.all_gather(amplitude_scale, 'event', axis=1, tiled=True)  42.8 us
    psum x1, waiting for transfers between devices, shards(): fields = lax.psum(partial_fields, 'wave')  42.8 us
    all_gather x1, waiting for transfers between devices, shards(): lax.all_gather(length, 'event', axis=1, tiled=True)  40.5 us
    dot_general x16, matrix products, forward(): jnp.dot(onehot, amp_rows, preferred_element_type=jnp.float32)  27.7 us
  transfers between devices with their start and end apart: 5, of which 4 were waited for; matrix products, arithmetic and copies ran while one was open for 14% of the time, Pallas kernels for 0%

commit v1 on v0

v1 whole, which is shorter than its diff:
```python
import math

import jax
import jax.numpy as jnp
from jax import lax
from jax.experimental import pallas as pl
from jax.experimental.pallas import tpu as pltpu
from jax.sharding import PartitionSpec as P

F32 = jnp.float32
BF16 = jnp.bfloat16

S, WL, R, B, E, G, NW = 8, 128, 64, 2048, 32768, 32, 4
NX = 4
TB = 256
NB = B // TB
NT = NB + NB * (NB - 1) // 2
IN_ROWS = 24
T = 512
Q = E // NX
HQ = Q // 2
NWIN = 8
ROOT = math.sqrt(math.log2(math.e))
VMEM = pl.BlockSpec(memory_space=pltpu.VMEM)
SMEM = pl.BlockSpec(memory_space=pltpu.SMEM)
ANY = pl.BlockSpec(memory_space=pl.ANY)
PARAMS = pltpu.CompilerParams(vmem_limit_bytes=56 * 1024 * 1024)


def low_lanes(shape):
    return lax.broadcasted_iota(jnp.int32, shape, len(shape) - 1) < 64


def swap(x):
    return pltpu.roll(x, 64, 1)


def pack_kernel(lat_ref, len_ref, amp_ref, out_ref):
    def rows(ref, qh):
        a = ref[pl.ds(qh * G, G), :]
        b = ref[pl.ds((qh + 2) * G, G), :]
        return jnp.concatenate([a.astype(F32), b.astype(F32)], axis=1)

    for qh in range(2):
        for s in range(S):
            out_ref[pl.ds(qh * S + s, G, stride=IN_ROWS), :] = rows(lat_ref.at[s], qh)
        out_ref[pl.ds(16 + qh * 2, G, stride=IN_ROWS), :] = rows(len_ref, qh)
        out_ref[pl.ds(17 + qh * 2, G, stride=IN_ROWS), :] = rows(amp_ref, qh)
    for r in range(20, IN_ROWS):
        out_ref[pl.ds(r, G, stride=IN_ROWS), :] = jnp.zeros((G, 128), F32)


def split_pair(a, b):
    low = low_lanes(a.shape)
    return jnp.where(low, a, swap(b)), jnp.where(low, swap(a), b)


def put_vectors(x_ref, q, k, vec):
    hi = vec.astype(BF16)
    lo = (vec - hi.astype(F32)).astype(BF16)
    x_ref[q, k // 2, :, (k % 2) * 128 : (k % 2) * 128 + 128] = jnp.concatenate([hi, lo], axis=0)


def times_tile(x_ref, y_ref, q, i, j, tile, both):
    y_ref[q, j] += jnp.dot(x_ref[q, i], tile, preferred_element_type=F32)
    if both:
        y_ref[q, i] += lax.dot_general(
            x_ref[q, j], tile, (((1,), (1,)), ((), ())), preferred_element_type=F32
        )


def tile_place(t):
    i = t & (NB - 1)
    return i, (i + (t >> 3)) & (NB - 1)


def send_rows(y_ref, scale_ref, out_ref):
    for k in range(B // 128):
        def part(q):
            y = y_ref[q, k // 2, :, (k % 2) * 128 : (k % 2) * 128 + 128]
            return (y[0:8] + y[8:16]) * scale_ref[q : q + 1, k * 128 : k * 128 + 128]

        first, second = [], []
        for qh in range(2):
            a, b = split_pair(part(qh), part(qh + 2))
            first.append(a)
            second.append(b)
        out_ref[32 * k : 32 * k + 16, :] = jnp.concatenate(first, axis=0).astype(out_ref.dtype)
        out_ref[32 * k + 16 : 32 * k + 32, :] = jnp.concatenate(second, axis=0).astype(out_ref.dtype)


def gen_kernel(r_ref, xy_ref, kern_ref, amp_ref, scale_ref, store, la, x_ref, y_ref, sq_row, sq_col, xy_row, xy_col, dist, sem):
    scale_ref[...] = jnp.zeros_like(scale_ref)
    for k in range(B // 128):
        lanes = slice(k * 128, k * 128 + 128)
        base = 2 * k * IN_ROWS
        pair = split_pair(r_ref[base + 16 : base + 24, :], r_ref[base + IN_ROWS + 16 : base + IN_ROWS + 24, :])
        for h in range(2):
            la[h, :, lanes] = pair[h]
        for c in range(2):
            row = xy_ref[c : c + 1, lanes] * ROOT
            wide = jnp.broadcast_to(row, (128, 128))
            xy_row[c, k // 2, :, (k % 2) * 128 : (k % 2) * 128 + 128] = wide[0:8]
            xy_col[c, lanes, :] = wide.T
    for h in range(2):
        for qh in range(2):
            q = qh + 2 * h
            length = la[h, 2 * qh : 2 * qh + 1, :]
            amp = la[h, 2 * qh + 1 : 2 * qh + 2, :]
            scale_ref[q : q + 1, :] = amp * jnp.sqrt(length * math.sqrt(2.0))
            la[h, 2 * qh : 2 * qh + 1, :] = length * length
    for k in range(B // 128):
        lanes = slice(k * 128, k * 128 + 128)
        base = 2 * k * IN_ROWS
        for qh in range(2):
            pair = split_pair(
                r_ref[base + 8 * qh : base + 8 * qh + 8, :],
                r_ref[base + IN_ROWS + 8 * qh : base + IN_ROWS + 8 * qh + 8, :],
            )
            for h in range(2):
                q = qh + 2 * h
                put_vectors(x_ref, q, k, pair[h] * scale_ref[q : q + 1, lanes])
                wide = jnp.broadcast_to(la[h, 2 * qh : 2 * qh + 1, lanes], (128, 128))
                sq_row[q, k // 2, :, (k % 2) * 128 : (k % 2) * 128 + 128] = wide[0:8]
                sq_col[q, lanes, :] = wide.T
    y_ref[...] = jnp.zeros_like(y_ref)

    step = 32

    def tile(t, both):
        i, j = tile_place(t)
        row0 = pl.multiple_of(i * TB, TB)
        for st in range(TB // step):
            rows = pl.ds(row0 + st * step, step)
            xc = xy_col[0, rows, :].reshape(step // 8, 8, 128)
            yc = xy_col[1, rows, :].reshape(step // 8, 8, 128)
            for c in range(2):
                half = slice(c * 128, c * 128 + 128)
                dx = xc - xy_row[0, j, :, half][None]
                dy = yc - xy_row[1, j, :, half][None]
                d = -(dx * dx) - dy * dy
                dist[st * step : st * step + step, half] = d.reshape(step, 128)
        for q in range(NW):
            for st in range(TB // step):
                sq = sq_col[q, pl.ds(row0 + st * step, step), :].reshape(step // 8, 8, 128)
                parts = []
                for c in range(2):
                    half = slice(c * 128, c * 128 + 128)
                    root = lax.rsqrt(sq + sq_row[q, j, :, half][None])
                    d = dist[st * step : st * step + step, half].reshape(step // 8, 8, 128)
                    parts.append((root * jnp.exp2(root * root * d)).reshape(step, 128).astype(BF16))
                store[t, q, st * step : st * step + step, :] = jnp.concatenate(parts, axis=1)
            times_tile(x_ref, y_ref, q, i, j, store[t, q], both)
        pltpu.make_async_copy(store.at[t], kern_ref.at[t], sem).start()

    @pl.loop(0, NB)
    def _(t):
        tile(t, False)

    @pl.loop(NB, NT)
    def _(t):
        tile(t, True)

    send_rows(y_ref, scale_ref, amp_ref)
    pltpu.make_async_copy(store, kern_ref, sem).wait()


def pull_kernel(g_ref, scale_ref, kern_ref, out_ref, store, x_ref, y_ref, sems):
    for t in range(NT):
        pltpu.make_async_copy(kern_ref.at[t], store.at[t], sems.at[t]).start()
    for k in range(B // 128):
        lanes = slice(k * 128, k * 128 + 128)
        a = g_ref[32 * k : 32 * k + 16, :].astype(F32)
        b = g_ref[32 * k + 16 : 32 * k + 32, :].astype(F32)
        pair = split_pair(a, b)
        for h in range(2):
            for qh in range(2):
                q = qh + 2 * h
                put_vectors(x_ref, q, k, pair[h][8 * qh : 8 * qh + 8] * scale_ref[q : q + 1, lanes])
    y_ref[...] = jnp.zeros_like(y_ref)

    def tile(t, both):
        i, j = tile_place(t)
        pltpu.make_async_copy(kern_ref.at[t], store.at[t], sems.at[t]).wait()
        for q in range(NW):
            times_tile(x_ref, y_ref, q, i, j, store[t, q], both)

    @pl.loop(0, NB)
    def _(t):
        tile(t, False)

    @pl.loop(NB, NT)
    def _(t):
        tile(t, True)

    send_rows(y_ref, scale_ref, out_ref)


def window_bins(first, shape):
    return first + lax.broadcasted_iota(jnp.int32, shape, 0)


def forward_kernel(me_ref, bins_ref, seg_ref, amp_ref, basis_ref, out0, out1, out2, out3, rows_ref, table, psi, acc, sems):
    me = me_ref[0]

    def place(k, m):
        return pl.multiple_of(((me + k) & (NX - 1)) * Q + m * 1024, 1024)

    def copies(k, m):
        return [
            pltpu.make_async_copy(
                basis_ref.at[pl.ds(place(k, m) + half * HQ, 1024), :],
                psi.at[k * 4 + m, pl.ds(half * 1024, 1024), :],
                sems.at[k * 4 + m, half],
            )
            for half in range(2)
        ]

    @pl.loop(0, 16)
    def _(c):
        for one in copies(c >> 2, c & 3):
            one.start()

    rows_ref[...] = amp_ref[...].astype(F32)
    table[...] = jnp.zeros_like(table)
    low = low_lanes((64, 128))
    for s in range(0, S, 2):
        stack = [rows_ref[pl.ds(qh * S + s + d, G, stride=16), :] for d in range(2) for qh in range(2)]
        flipped = jnp.concatenate(stack, axis=0).T
        top, bottom = flipped[0:64], flipped[64:128]
        table[pl.ds(s, R, stride=S), :] = jnp.where(low, top, swap(bottom))
        table[pl.ds(s + 1, R, stride=S), :] = jnp.where(low, swap(top), bottom)

    for k, out_ref in enumerate((out0, out1, out2, out3)):

        @pl.loop(0, 4)
        def _(m):
            c = k * 4 + m
            for one in copies(k, m):
                one.wait()
            places = [(u, half, place(k, m) + half * HQ + u * T) for u in range(2) for half in range(2)]

            def select(u, half, event, first, start):
                window = table[pl.ds(pl.multiple_of(first * S, S), NWIN * S), :].astype(BF16)
                values = psi[c, half * 1024 + u * T : half * 1024 + u * T + T, :]
                fields = lax.dot_general(
                    window, values, (((1,), (1,)), ((), ())), preferred_element_type=F32
                )
                seg = jnp.broadcast_to(seg_ref[0:1, pl.ds(pl.multiple_of(event, T), T)], (S, T)) - first
                for g in range(NWIN):
                    start = jnp.where(seg == g, fields[g * S : g * S + S], start)
                return start

            spans = []
            for u, half, event in places:
                first = bins_ref[0, event]
                acc[u, half * S : half * S + S, :] = select(u, half, event, first, jnp.zeros((S, T), F32))
                spans.append(bins_ref[0, event + T - 1] - first)
            widest = jnp.maximum(jnp.maximum(spans[0], spans[1]), jnp.maximum(spans[2], spans[3]))

            @pl.when(widest >= NWIN)
            def _():
                for (u, half, event), span in zip(places, spans):
                    first = bins_ref[0, event]

                    @pl.loop(1, span // NWIN + 1)
                    def _(w):
                        old = acc[u, half * S : half * S + S, :]
                        acc[u, half * S : half * S + S, :] = select(u, half, event, first + w * NWIN, old)

            for u in range(2):
                out_ref[:, pl.ds(pl.multiple_of(m * 1024 + u * T, T), T)] = acc[u].astype(BF16)


def weight_kernel(a_ref, b_ref, c_ref, d_ref, out_ref):
    field = (a_ref[...].astype(F32) + b_ref[...].astype(F32)) + (c_ref[...].astype(F32) + d_ref[...].astype(F32))
    out_ref[...] = (-2.0 / S * field / (1.0 + field * field)).astype(BF16)


def backward_kernel(me_ref, bins_ref, w0_ref, w1_ref, w2_ref, w3_ref, seg_ref, amp_ref, norm_ref, basis_ref, out_ref, rows_ref, sums, psi, sems):
    me = me_ref[0]

    def place(k, m):
        return pl.multiple_of(((me - k) & (NX - 1)) * Q + m * 1024, 1024)

    def copies(k, m):
        return [
            pltpu.make_async_copy(
                basis_ref.at[pl.ds(place(k, m) + half * HQ, 1024), :],
                psi.at[k * 4 + m, pl.ds(half * 1024, 1024), :],
                sems.at[k * 4 + m, half],
            )
            for half in range(2)
        ]

    @pl.loop(0, 16)
    def _(c):
        for one in copies(c >> 2, c & 3):
            one.start()

    sums[...] = jnp.zeros_like(sums)
    for k, w_ref in enumerate((w0_ref, w1_ref, w2_ref, w3_ref)):

        @pl.loop(0, 4)
        def _(m):
            c = k * 4 + m
            for one in copies(k, m):
                one.wait()
            places = [(u, half, place(k, m) + half * HQ + u * T) for u in range(2) for half in range(2)]

            def add(u, half, event, first):
                weight = w_ref[:, pl.ds(pl.multiple_of(m * 1024 + u * T, T), T)].astype(F32)
                weight = weight[half * S : half * S + S]
                values = psi[c, half * 1024 + u * T : half * 1024 + u * T + T, :]
                seg = jnp.broadcast_to(seg_ref[0:1, pl.ds(pl.multiple_of(event, T), T)], (S, T)) - first
                spread = jnp.concatenate([jnp.where(seg == g, weight, 0.0) for g in range(NWIN)], axis=0)
                added = jnp.dot(spread.astype(BF16), values, preferred_element_type=F32)
                sums[pl.ds(pl.multiple_of(first * S, S), NWIN * S), :] += added

            spans = []
            for u, half, event in places:
                first = bins_ref[0, event]
                add(u, half, event, first)
                spans.append(bins_ref[0, event + T - 1] - first)
            widest = jnp.maximum(jnp.maximum(spans[0], spans[1]), jnp.maximum(spans[2], spans[3]))

            @pl.when(widest >= NWIN)
            def _():
                for (u, half, event), span in zip(places, spans):
                    first = bins_ref[0, event]

                    @pl.loop(1, span // NWIN + 1)
                    def _(w):
                        add(u, half, event, first + w * NWIN)

    rows_ref[...] = amp_ref[...].astype(F32)
    norm = [
        jnp.concatenate([norm_ref[pl.ds(qh * G, G), :], norm_ref[pl.ds((qh + 2) * G, G), :]], axis=1) * (2.0 / S)
        for qh in range(2)
    ]
    low = low_lanes((G, 128))
    for s in range(0, S, 2):
        stack = [sums[pl.ds(s + d, R, stride=S), :] for d in range(2)]
        flipped = jnp.concatenate(stack, axis=0).T
        for qh in range(2):
            a, b = flipped[qh * G : qh * G + G], flipped[(qh + 2) * G : (qh + 2) * G + G]
            parts = (jnp.where(low, a, swap(b)), jnp.where(low, swap(a), b))
            for d in range(2):
                where = pl.ds(qh * S + s + d, G, stride=16)
                rows_ref[where, :] = rows_ref[where, :] * norm[qh] + parts[d]
    out_ref[...] = rows_ref[...].astype(BF16)


def unpack_kernel(r_ref, lat_ref, out_ref):
    for qh in range(2):
        for s in range(S):
            v = r_ref[pl.ds(qh * S + s, G, stride=16), :]
            for h in range(2):
                where = pl.ds((qh + 2 * h) * G, G)
                out_ref[s, where, :] = v[:, h * 64 : h * 64 + 64] + lat_ref[s, where, :].astype(F32)


def struct(shape, dtype):
    return jax.ShapeDtypeStruct(shape, dtype)


def exchange(x, rows):
    y = lax.all_to_all(x.reshape(G, rows, 128), "event", 0, 0)
    return y.reshape(G * rows, 128)


def shift(x, k):
    return lax.ppermute(x, "wave", [(i, (i + k) % NX) for i in range(NX)])


def shards(latent, basis, event_bin, length, amplitude_scale, yield_norm, bin_coords):
    me = lax.axis_index("wave").astype(jnp.int32).reshape(1)
    packed = pl.pallas_call(
        pack_kernel,
        out_shape=struct((G * IN_ROWS, 128), F32),
        in_specs=[VMEM] * 3,
        out_specs=VMEM,
        name="pack",
    )(latent, length, amplitude_scale)
    arrived = exchange(packed, IN_ROWS)
    kern, amp_out, scale = pl.pallas_call(
        gen_kernel,
        out_shape=(
            struct((NT, NW, TB, TB), BF16),
            struct((G * 16, 128), BF16),
            struct((8, B), F32),
        ),
        in_specs=[VMEM] * 2,
        out_specs=(ANY, VMEM, VMEM),
        scratch_shapes=[
            pltpu.VMEM((NT, NW, TB, TB), BF16),
            pltpu.VMEM((2, 8, B), F32),
            pltpu.VMEM((NW, NB, 16, TB), BF16),
            pltpu.VMEM((NW, NB, 16, TB), F32),
            pltpu.VMEM((NW, NB, 8, TB), F32),
            pltpu.VMEM((NW, B, 128), F32),
            pltpu.VMEM((2, NB, 8, TB), F32),
            pltpu.VMEM((2, B, 128), F32),
            pltpu.VMEM((TB, TB), F32),
            pltpu.SemaphoreType.DMA,
        ],
        compiler_params=PARAMS,
        name="gen",
    )(arrived, bin_coords)
    amp_in = exchange(amp_out, 16)
    fields = pl.pallas_call(
        forward_kernel,
        out_shape=[struct((2 * S, HQ), BF16)] * NX,
        in_specs=[SMEM, SMEM, VMEM, VMEM, ANY],
        out_specs=[VMEM] * NX,
        scratch_shapes=[
            pltpu.VMEM((G * 16, 128), F32),
            pltpu.VMEM(((R + NWIN) * S, 128), F32),
            pltpu.VMEM((16, 2048, 128), BF16),
            pltpu.VMEM((2, 2 * S, T), F32),
            pltpu.SemaphoreType.DMA((16, 2)),
        ],
        compiler_params=PARAMS,
        name="forward",
    )(me, event_bin, event_bin, amp_in, basis)
    others = [shift(fields[k], k) for k in range(1, NX)]
    weight = pl.pallas_call(
        weight_kernel,
        out_shape=struct((2 * S, HQ), BF16),
        in_specs=[VMEM] * 4,
        out_specs=VMEM,
        name="weight",
    )(fields[0], *others)
    weights = [weight] + [shift(weight, k) for k in range(1, NX)]
    grad_out = pl.pallas_call(
        backward_kernel,
        out_shape=struct((G * 16, 128), BF16),
        in_specs=[SMEM, SMEM] + [VMEM] * 7 + [ANY],
        out_specs=VMEM,
        scratch_shapes=[
            pltpu.VMEM((G * 16, 128), F32),
            pltpu.VMEM(((R + NWIN) * S, 128), F32),
            pltpu.VMEM((16, 2048, 128), BF16),
            pltpu.SemaphoreType.DMA((16, 2)),
        ],
        compiler_params=PARAMS,
        name="backward",
    )(me, event_bin, *weights, event_bin, amp_in, yield_norm, basis)
    grad_in = exchange(grad_out, 16)
    pulled = pl.pallas_call(
        pull_kernel,
        out_shape=struct((G * 16, 128), F32),
        in_specs=[VMEM, VMEM, ANY],
        out_specs=VMEM,
        scratch_shapes=[
            pltpu.VMEM((NT, NW, TB, TB), BF16),
            pltpu.VMEM((NW, NB, 16, TB), BF16),
            pltpu.VMEM((NW, NB, 16, TB), F32),
            pltpu.SemaphoreType.DMA((NT,)),
        ],
        compiler_params=PARAMS,
        name="pull",
    )(grad_in, scale, kern)
    back = exchange(pulled, 16)
    return pl.pallas_call(
        unpack_kernel,
        out_shape=struct((S, WL, R), F32),
        in_specs=[VMEM] * 2,
        out_specs=VMEM,
        name="unpack",
    )(back, latent)


def solution(mesh):
    placed = (
        P(None, "wave", "event"),
        P("event", "wave"),
        P("event", None),
        P("wave", "event"),
        P("wave", "event"),
        P("wave", "event"),
        P(),
    )
    return jax.shard_map(
        shards, mesh=mesh, in_specs=placed, out_specs=P(None, "wave", "event"), check_vma=False
    )
```

time: 616 us -> 148 us (0.24)
  other arithmetic: 243 us -> 0 us
  waiting for transfers between devices: 177 us -> 15.6 us
  matrix products: 112 us -> 0 us
  Pallas kernels: 0 us -> 60.4 us
  local copies, waits for them, and re-layouts: 65.6 us -> 10.7 us
  blocking collectives: 0 us -> 47.8 us
  between operations: 13.3 us -> 0.07 us
  starting transfers between devices: 0.34 us -> 12.8 us
    convert_element_type x49 -> x0, other arithmetic: 158 us -> none  [the longest x16 138 us: backward(): (weight.T[:, :, None] * psi.astype(jnp.float32)[:, None, :]).astype(jnp.b...]
    all_gather x4 -> x0, waiting for transfers between devices: 133 us -> none  [the longest x1 49.2 us: shards(): piece = lax.all_gather(grad_rows, 'event', axis=0, tiled=True)]
    dot_general x34 -> x0, matrix products: 112 us -> none  [the longest x16 53 us: backward(): lax.dot_general(onehot, terms, (((0,), (0,)), ((), ())), preferred_elemen...]
    dynamic_update_slice x8 -> x0, other arithmetic: 66.3 us -> none  [shards(): lax.map(build, (split_waves(length), split_waves(amplitude_scale), split_...]
    pallas_call x0 -> x7, Pallas kernels: none -> 60.4 us  [the longest x1 22.1 us: shards(): pl.pallas_call(gen_kernel, out_shape=(struct((NT, NW, TB, TB), BF16), str...]
    all_to_all x0 -> x3, blocking collectives: none -> 47.8 us  [exchange(): y = lax.all_to_all(x.reshape(G, rows, 128), 'event', 0, 0)]
    psum x1 -> x0, waiting for transfers between devices: 42.8 us -> none  [shards(): fields = lax.psum(partial_fields, 'wave')]
    dynamic_slice x65 -> x0, local copies, waits for them, and re-layouts: 21.8 us -> none  [the longest x64 21 us: shards(): partial_fields = lax.map(forward, (basis_blocks, bin_blocks))]
  transfers between devices with their start and end apart: 5 -> 7, of which waited for: 4 -> 5; matrix products, arithmetic and copies ran while one was open for 14% -> 1% of each run, Pallas kernels for 0% -> 0%
where the time goes in v1:
time: 148 us; the launch traced here: 147 us
  Pallas kernels  60.4 us (41%)
  blocking collectives  47.8 us (32%)
  waiting for transfers between devices  15.6 us (11%)
  starting transfers between devices  12.8 us (9%)
  local copies, waits for them, and re-layouts  10.7 us (7%)
    all_to_all x3, blocking collectives, exchange(): y = lax.all_to_all(x.reshape(G, rows, 128), 'event', 0, 0)  47.8 us
    pallas_call x1, Pallas kernels, shards(): pl.pallas_call(gen_kernel, out_shape=(struct((NT, NW, TB, TB), BF16), str...  22.1 us
    pallas_call x1, Pallas kernels, shards(): pl.pallas_call(pull_kernel, out_shape=struct((G * 16, 128), F32), in_spec...  13.8 us
    pallas_call x1, Pallas kernels, shards(): pl.pallas_call(forward_kernel, out_shape=[struct((2 * S, HQ), BF16)] * NX...  9.88 us
    ppermute x6, starting transfers between devices, shift(): return lax.ppermute(x, 'wave', [(i, (i + k) % NX) for i in range(NX)])  8.97 us
    pallas_call x1, Pallas kernels, shards(): pl.pallas_call(backward_kernel, out_shape=struct((G * 16, 128), BF16), in...  8.89 us
    unnamed x18, local copies, waits for them, and re-layouts  8.82 us
    ppermute x6, waiting for transfers between devices, shift(): return lax.ppermute(x, 'wave', [(i, (i + k) % NX) for i in range(NX)])  7.82 us
  transfers between devices with their start and end apart: 7, of which 5 were waited for; matrix products, arithmetic and copies ran while one was open for 1% of the time, Pallas kernels for 0%

profile of v1, /device:TPU:1, one launch (start us, length us, event | category | flops | bytes accessed | tf_op | source)
XLA Modules:
  0.0 147.5 jit_solution(12675787141265860614)
XLA Ops:
  0.0 1.7 %copy.8.lat_ref = bf16[8,128,64]{2,1,0:T(8,128)(2,1)} copy(bf16[8,128,64]{1,2,0:T(8,128)(2,1)} %param.7) | data formatting | bytes 262144 | tf_op args[0]
  1.7 1.5 %copy.10.amp_ref = f32[128,64]{1,0:T(8,128)} copy(f32[128,64]{0,1:T(8,128)} %param.11) | data formatting | bytes 65536 | tf_op args[4]
  3.2 1.5 copy.9.len_ref
  4.7 1.9 %pack.1 = f32[768,128]{1,0:T(8,128)} custom-call(bf16[8,128,64]{2,1,0:T(8,128)(2,1)} %copy.8.lat_ref, f32[128,64]{1,0:T(8,128)} %copy.9.len_ref, f32[128,64]{1,0:T(8,128)} %copy.10.amp_ref), custom_call_target="tpu_custom_call" | custom-call | tf_op jit(solution)/shard_map/pack/pallas_call | solution.py:378
  6.6 19.9 %all_to_all.20 = f32[32,24,128]{2,1,0:T(8,128)} all-to-all(f32[32,24,128]{2,1,0:T(8,128)} %bitcast.10), channel_id=1, replica_groups=mesh['wave'=4,'event'=32] {'event'}, dimensions={0} | all-to-all | bytes 786432 | tf_op jit(solution)/shard_map/all_to_all | solution.py:368
  26.4 22.1 %gen.1 = (bf16[36,4,256,256]{3,2,1,0:T(8,128)(2,1)}, bf16[512,128]{1,0:T(8,128)(2,1)}, f32[8,2048]{1,0:T(8,128)}) custom-call(f32[768,128]{1,0:T(8,128)} %bitcast.9, f32[2,2048]{1,0:T(2,128)} %xy_ref.1), custom_call_target="tpu_custom_call" | custom-call | tf_op jit(solution)/shard_map/gen/pallas_call | solution.py:386
  48.5 3.9 %all-to-all-start.1 = ((bf16[32,16,128]{2,1,0:T(8,128)(2,1)}), bf16[32,16,128]{2,1,0:T(8,128)(2,1)S(1)}, u32[]{:S(2)}, u32[]{:S(2)}) async-start(bf16[32,16,128]{2,1,0:T(8,128)(2,1)} %bitcast.17), calls=%async_computation.1 | async-start | bytes 262144 | tf_op jit(solution)/shard_map/all_to_all | solution.py:368
  52.4 7.7 %all-to-all-done.1 = bf16[32,16,128]{2,1,0:T(8,128)(2,1)S(1)} async-done(((bf16[32,16,128]{2,1,0:T(8,128)(2,1)}), bf16[32,16,128]{2,1,0:T(8,128)(2,1)S(1)}, u32[]{:S(2)}, u32[]{:S(2)}) %all-to-all-start.1) | async-done | bytes 131104 | tf_op jit(solution)/shard_map/all_to_all | solution.py:368
  60.8 9.9 %forward.1 = (bf16[16,4096]{1,0:T(8,128)(2,1)}, bf16[16,4096]{1,0:T(8,128)(2,1)}, bf16[16,4096]{1,0:T(8,128)(2,1)}, bf16[16,4096]{1,0:T(8,128)(2,1)}) custom-call(s32[1]{0:T(128)} %bitcast.me_ref, s32[1,32768]{1,0:T(1,128)} %seg_ref.3, s32[1,32768]{1,0:T(1,128)} %seg_ref.3, bf16[512,128]{1,0:T(8,128)(2,1)} %bitcast.11, bf16[32768,128]{1,0:T(8,128)(2,1)} %basis_ref.3), custom_call_target="tpu_custom_call" | custom-call | tf_op jit(solution)/shard_map/forward/pallas_call | solution.py:411
  70.7 1.3 collective-permute-start
  72.0 2.5 %collective-permute-start.1 = (bf16[16,4096]{1,0:T(8,128)(2,1)}, bf16[16,4096]{1,0:T(8,128)(2,1)S(1)}, u32[]{:S(2)}, u32[]{:S(2)}) collective-permute-start(bf16[16,4096]{1,0:T(8,128)(2,1)} %get-tuple-element.15), channel_id=1, source_target_pairs={{0,64},{32,96},{64,0},{96,32},{1,65},{33,97},{65,1},{97,33},{2,66}... | collective-permute-start | bytes 393224 | tf_op jit(solution)/shard_map/ppermute | solution.py:373
  74.4 1.1 collective-permute-start.2
  75.6 1.3 collective-permute-done.b_ref
  76.8 3.8 %collective-permute-done.1.c_ref = bf16[16,4096]{1,0:T(8,128)(2,1)S(1)} collective-permute-done((bf16[16,4096]{1,0:T(8,128)(2,1)}, bf16[16,4096]{1,0:T(8,128)(2,1)S(1)}, u32[]{:S(2)}, u32[]{:S(2)}) %collective-permute-start.1) | collective-permute-done | bytes 131104 | tf_op jit(solution)/shard_map/ppermute | solution.py:373
  81.4 1.9 %weight.1.w0_ref = bf16[16,4096]{1,0:T(8,128)(2,1)} custom-call(bf16[16,4096]{1,0:T(8,128)(2,1)} %get-tuple-element.13.a_ref, bf16[16,4096]{1,0:T(8,128)(2,1)} %copy-done.4, bf16[16,4096]{1,0:T(8,128)(2,1)} %copy-done.5, bf16[16,4096]{1,0:T(8,128)(2,1)} %copy-done.6), custom_call_target="tpu_custom_call" | custom-call | tf_op jit(solution)/shard_map/weight/pallas_call | solution.py:427
  84.2 2.2 %collective-permute-start.4 = (bf16[16,4096]{1,0:T(8,128)(2,1)}, bf16[16,4096]{1,0:T(8,128)(2,1)S(1)}, u32[]{:S(2)}, u32[]{:S(2)}) collective-permute-start(bf16[16,4096]{1,0:T(8,128)(2,1)} %weight.1.w0_ref), channel_id=1, source_target_pairs={{0,64},{32,96},{64,0},{96,32},{1,65},{33,97},{65,1},{97,33},{2,66}... | collective-permute-start | bytes 393224 | tf_op jit(solution)/shard_map/ppermute | solution.py:373
  87.4 1.5 %copy.11.norm_ref = f32[128,64]{1,0:T(8,128)} copy(f32[128,64]{0,1:T(8,128)} %param.12) | data formatting | bytes 65536 | tf_op args[5]
  88.9 2.7 %collective-permute-done.4.w2_ref = bf16[16,4096]{1,0:T(8,128)(2,1)S(1)} collective-permute-done((bf16[16,4096]{1,0:T(8,128)(2,1)}, bf16[16,4096]{1,0:T(8,128)(2,1)S(1)}, u32[]{:S(2)}, u32[]{:S(2)}) %collective-permute-start.4) | collective-permute-done | bytes 131104 | tf_op jit(solution)/shard_map/ppermute | solution.py:373
  92.8 8.9 %backward.1 = bf16[512,128]{1,0:T(8,128)(2,1)} custom-call(s32[1]{0:T(128)} %bitcast.me_ref, s32[1,32768]{1,0:T(1,128)} %seg_ref.3, bf16[16,4096]{1,0:T(8,128)(2,1)} %weight.1.w0_ref, bf16[16,4096]{1,0:T(8,128)(2,1)} %copy-done.1, bf16[16,4096]{1,0:T(8,128)(2,1)} %copy-done.2, bf16[16,4096]{1,0:T(8,128)(2,1)} %copy-done.3, s32[1,32768]{1,0:T(1,128)} %seg_ref.3, ...), custom_call_target="tpu_custom_call" | custom-call | tf_op jit(solution)/shard_map/backward/pallas_call | solution.py:435
  101.7 14.3 %all_to_all.21 = bf16[32,16,128]{2,1,0:T(8,128)(2,1)} all-to-all(bf16[32,16,128]{2,1,0:T(8,128)(2,1)} %bitcast.15), channel_id=1, replica_groups=mesh['wave'=4,'event'=32] {'event'}, dimensions={0} | all-to-all | bytes 262144 | tf_op jit(solution)/shard_map/all_to_all | solution.py:368
  116.0 13.8 %pull.1 = f32[512,128]{1,0:T(8,128)} custom-call(bf16[512,128]{1,0:T(8,128)(2,1)} %bitcast.16, f32[8,2048]{1,0:T(8,128)} %get-tuple-element.17.scale_ref, bf16[36,4,256,256]{3,2,1,0:T(8,128)(2,1)} %get-tuple-element.18.kern_ref), custom_call_target="tpu_custom_call" | custom-call | tf_op jit(solution)/shard_map/pull/pallas_call | solution.py:450
  129.8 13.6 %all_to_all.22 = f32[32,16,128]{2,1,0:T(8,128)} all-to-all(f32[32,16,128]{2,1,0:T(8,128)} %bitcast.13), channel_id=1, replica_groups=mesh['wave'=4,'event'=32] {'event'}, dimensions={0} | all-to-all | bytes 524288 | tf_op jit(solution)/shard_map/all_to_all | solution.py:368
  143.5 2.0 %unpack.1 = f32[8,128,64]{2,1,0:T(8,128)} custom-call(f32[512,128]{1,0:T(8,128)} %bitcast.14, bf16[8,128,64]{2,1,0:T(8,128)(2,1)} %copy.8.lat_ref), custom_call_target="tpu_custom_call" | custom-call | tf_op jit(solution)/shard_map/unpack/pallas_call | solution.py:465
  145.5 1.9 %copy.13 = f32[8,128,64]{1,2,0:T(8,128)} copy(f32[8,128,64]{2,1,0:T(8,128)} %unpack.1) | data formatting | bytes 524288 | tf_op jit(solution)/shard_map/unpack/pallas_call | solution.py:465
  (19 shorter events, 4.6 us)
Async XLA Ops:
  48.5 11.6 %all-to-all-start.1 = ((bf16[32,16,128]{2,1,0:T(8,128)(2,1)}), bf16[32,16,128]{2,1,0:T(8,128)(2,1)S(1)}, u32[]{:S(2)}, u32[]{:S(2)}) async-start(bf16[32,16,128]{2,1,0:T(8,128)(2,1)} %bitcast.17), calls=%async_computation.1 | async-start | bytes 262144 | tf_op jit(solution)/shard_map/all_to_all | solution.py:368
  60.1 0.7 copy-start
  70.7 6.2 %collective-permute-start = (bf16[16,4096]{1,0:T(8,128)(2,1)}, bf16[16,4096]{1,0:T(8,128)(2,1)S(1)}, u32[]{:S(2)}, u32[]{:S(2)}) collective-permute-start(bf16[16,4096]{1,0:T(8,128)(2,1)} %get-tuple-element.14), channel_id=1, source_target_pairs={{0,32},{32,64},{64,96},{96,0},{1,33},{33,65},{65,97},{97,1},{2,34}... | collective-permute-start | bytes 393224 | tf_op jit(solution)/shard_map/ppermute | solution.py:373
  72.0 8.7 %collective-permute-start.1 = (bf16[16,4096]{1,0:T(8,128)(2,1)}, bf16[16,4096]{1,0:T(8,128)(2,1)S(1)}, u32[]{:S(2)}, u32[]{:S(2)}) collective-permute-start(bf16[16,4096]{1,0:T(8,128)(2,1)} %get-tuple-element.15), channel_id=1, source_target_pairs={{0,64},{32,96},{64,0},{96,32},{1,65},{33,97},{65,1},{97,33},{2,66}... | collective-permute-start | bytes 393224 | tf_op jit(solution)/shard_map/ppermute | solution.py:373
  74.4 6.2 %collective-permute-start.2 = (bf16[16,4096]{1,0:T(8,128)(2,1)}, bf16[16,4096]{1,0:T(8,128)(2,1)S(1)}, u32[]{:S(2)}, u32[]{:S(2)}) collective-permute-start(bf16[16,4096]{1,0:T(8,128)(2,1)} %get-tuple-element.16), channel_id=1, source_target_pairs={{0,96},{32,0},{64,32},{96,64},{1,97},{33,1},{65,33},{97,65},{2,98}... | collective-permute-start | bytes 393224 | tf_op jit(solution)/shard_map/ppermute | solution.py:373
  76.8 3.9 %copy-start.4 = (bf16[16,4096]{1,0:T(8,128)(2,1)}, bf16[16,4096]{1,0:T(8,128)(2,1)S(1)}, u32[]{:S(2)}) copy-start(bf16[16,4096]{1,0:T(8,128)(2,1)S(1)} %collective-permute-done.b_ref) | copy-start | bytes 393220
  80.7 0.6 copy-start.5
  80.7 0.7 copy-start.6
  83.3 5.6 %collective-permute-start.3 = (bf16[16,4096]{1,0:T(8,128)(2,1)}, bf16[16,4096]{1,0:T(8,128)(2,1)S(1)}, u32[]{:S(2)}, u32[]{:S(2)}) collective-permute-start(bf16[16,4096]{1,0:T(8,128)(2,1)} %weight.1.w0_ref), channel_id=1, source_target_pairs={{0,32},{32,64},{64,96},{96,0},{1,33},{33,65},{65,97},{97,1},{2,34}... | collective-permute-start | bytes 393224 | tf_op jit(solution)/shard_map/ppermute | solution.py:373
  84.2 7.3 %collective-permute-start.4 = (bf16[16,4096]{1,0:T(8,128)(2,1)}, bf16[16,4096]{1,0:T(8,128)(2,1)S(1)}, u32[]{:S(2)}, u32[]{:S(2)}) collective-permute-start(bf16[16,4096]{1,0:T(8,128)(2,1)} %weight.1.w0_ref), channel_id=1, source_target_pairs={{0,64},{32,96},{64,0},{96,32},{1,65},{33,97},{65,1},{97,33},{2,66}... | collective-permute-start | bytes 393224 | tf_op jit(solution)/shard_map/ppermute | solution.py:373
  86.4 5.1 %collective-permute-start.5 = (bf16[16,4096]{1,0:T(8,128)(2,1)}, bf16[16,4096]{1,0:T(8,128)(2,1)S(1)}, u32[]{:S(2)}, u32[]{:S(2)}) collective-permute-start(bf16[16,4096]{1,0:T(8,128)(2,1)} %weight.1.w0_ref), channel_id=1, source_target_pairs={{0,96},{32,0},{64,32},{96,64},{1,97},{33,1},{65,33},{97,65},{2,98}... | collective-permute-start | bytes 393224 | tf_op jit(solution)/shard_map/ppermute | solution.py:373
  88.9 2.7 %copy-start.1 = (bf16[16,4096]{1,0:T(8,128)(2,1)}, bf16[16,4096]{1,0:T(8,128)(2,1)S(1)}, u32[]{:S(2)}) copy-start(bf16[16,4096]{1,0:T(8,128)(2,1)S(1)} %collective-permute-done.3.w1_ref) | copy-start | bytes 393220
  91.5 0.6 copy-start.2
  92.2 0.7 copy-start.3

commit v2 on v1

v2 whole, which is shorter than its diff:
```python
import math

import jax
import jax.numpy as jnp
from jax import lax
from jax.experimental import pallas as pl
from jax.experimental.pallas import tpu as pltpu
from jax.sharding import PartitionSpec as P

F32 = jnp.float32
BF16 = jnp.bfloat16

S, WL, R, B, E, G, NW = 8, 128, 64, 2048, 32768, 32, 4
NX = 4
SP = 4
TB = 256
NB = B // TB
NT = NB + NB * (NB - 1) // 2
IN_ROWS = 24
T = 512
TILES = E // T
Q = E // NX
HQ = Q // 2
NWIN = 8
ROOT = math.sqrt(math.log2(math.e))
VMEM = pl.BlockSpec(memory_space=pltpu.VMEM)
SMEM = pl.BlockSpec(memory_space=pltpu.SMEM)
ANY = pl.BlockSpec(memory_space=pl.ANY)


def low_lanes(shape):
    return lax.broadcasted_iota(jnp.int32, shape, len(shape) - 1) < 64


def swap(x):
    return pltpu.roll(x, 64, 1)


def pack_kernel(lat_hbm, len_hbm, amp_hbm, xy_hbm, out_ref, xy_ref, lat_ref, len_ref, amp_ref, rows, sems):
    copies = [
        pltpu.make_async_copy(source, target, sems.at[n])
        for n, (source, target) in enumerate(
            ((lat_hbm, lat_ref), (len_hbm, len_ref), (amp_hbm, amp_ref), (xy_hbm, xy_ref))
        )
    ]
    for one in copies:
        one.start()

    def put(row, value):
        for q in range(NW):
            rows[pl.ds(row(q), G, stride=IN_ROWS), :] = value[q * G : q * G + G]

    copies[0].wait()
    for sp in range(SP):
        pair = jnp.concatenate([lat_ref[sp], lat_ref[sp + SP]], axis=0).astype(F32)
        put(lambda q: q * SP + sp, pair.T)
    copies[1].wait()
    copies[2].wait()
    exact = jnp.concatenate([len_ref[...], amp_ref[...]], axis=0).T
    high = exact.astype(BF16).astype(F32)
    put(lambda q: 16 + q, high)
    put(lambda q: 20 + q, exact - high)
    out_ref[...] = rows[...].astype(BF16)
    copies[3].wait()


def split_pair(a, b):
    low = low_lanes(a.shape)
    return jnp.where(low, a, swap(b)), jnp.where(low, swap(a), b)


def put_vectors(x_ref, q, k, vec):
    hi = vec.astype(BF16)
    lo = (vec - hi.astype(F32)).astype(BF16)
    x_ref[q, k // 2, :, (k % 2) * 128 : (k % 2) * 128 + 128] = jnp.concatenate([hi, lo], axis=0)


def times_tile(x_ref, y_ref, q, i, j, tile, both):
    y_ref[q, j] += jnp.dot(x_ref[q, i], tile, preferred_element_type=F32)
    if both:
        y_ref[q, i] += lax.dot_general(
            x_ref[q, j], tile, (((1,), (1,)), ((), ())), preferred_element_type=F32
        )


def tile_place(t):
    i = t & (NB - 1)
    return i, (i + (t >> 3)) & (NB - 1)


def send_rows(y_ref, scale_ref, out_ref):
    for k in range(B // 128):
        parts = []
        for q in range(NW):
            y = y_ref[q, k // 2, :, (k % 2) * 128 : (k % 2) * 128 + 128]
            parts.append((y[0:8] + y[8:16]) * scale_ref[q : q + 1, k * 128 : k * 128 + 128])
        pair = split_pair(*(jnp.concatenate([y[s2 * SP : s2 * SP + SP] for y in parts], axis=0) for s2 in range(2)))
        for d in range(2):
            out_ref[32 * k + 16 * d : 32 * k + 16 * d + 16, :] = pair[d].astype(out_ref.dtype)


def take_vectors(first, second, k, x_ref, scale_ref):
    pair = split_pair(first, second)
    for q in range(NW):
        vec = jnp.concatenate([one[q * SP : q * SP + SP] for one in pair], axis=0)
        put_vectors(x_ref, q, k, vec * scale_ref[q : q + 1, k * 128 : k * 128 + 128])


def gen_kernel(
    r_ref, xy_ref, basis_hbm, bins_hbm, norm_hbm,
    kern_ref, amp_ref, scale_ref, psi_ref, seg_ref, norm_ref, edge_ref,
    rows_ref, la, x_ref, y_ref, sq_row, sq_col, xy_row, xy_col, dist, bins_ref, sems,
):
    copies = [
        pltpu.make_async_copy(source, target, sems.at[n])
        for n, (source, target) in enumerate(
            ((basis_hbm, psi_ref), (bins_hbm, seg_ref), (norm_hbm, norm_ref), (bins_hbm, bins_ref))
        )
    ]
    for one in copies:
        one.start()
    rows_ref[...] = r_ref[...].astype(F32)
    for k in range(B // 128):
        lanes = slice(k * 128, k * 128 + 128)
        base = 2 * k * IN_ROWS
        pair = split_pair(
            rows_ref[base + 16 : base + 24, :], rows_ref[base + IN_ROWS + 16 : base + IN_ROWS + 24, :]
        )
        for one in range(2):
            la[one, :, lanes] = pair[one]
        for c in range(2):
            row = xy_ref[c : c + 1, lanes] * ROOT
            wide = jnp.broadcast_to(row, (128, 128))
            xy_row[c, k // 2, :, (k % 2) * 128 : (k % 2) * 128 + 128] = wide[0:8]
            xy_col[c, lanes, :] = wide.T
    length = la[0, 0:NW, :] + la[0, NW : 2 * NW, :]
    amp = la[1, 0:NW, :] + la[1, NW : 2 * NW, :]
    scale_ref[NW:8, :] = jnp.zeros((8 - NW, B), F32)
    scale_ref[0:NW, :] = amp * jnp.sqrt(length * math.sqrt(2.0))
    la[0, 0:NW, :] = length * length
    for k in range(B // 128):
        lanes = slice(k * 128, k * 128 + 128)
        base = 2 * k * IN_ROWS
        take_vectors(
            rows_ref[base : base + 16, :], rows_ref[base + IN_ROWS : base + IN_ROWS + 16, :], k, x_ref, scale_ref
        )
        for q in range(NW):
            wide = jnp.broadcast_to(la[0, q : q + 1, lanes], (128, 128))
            sq_row[q, k // 2, :, (k % 2) * 128 : (k % 2) * 128 + 128] = wide[0:8]
            sq_col[q, lanes, :] = wide.T
    y_ref[...] = jnp.zeros_like(y_ref)

    step = 32

    def tile(t, both):
        i, j = tile_place(t)
        row0 = pl.multiple_of(i * TB, TB)
        for st in range(TB // step):
            rows = pl.ds(row0 + st * step, step)
            xc = xy_col[0, rows, :].reshape(step // 8, 8, 128)
            yc = xy_col[1, rows, :].reshape(step // 8, 8, 128)
            for c in range(2):
                half = slice(c * 128, c * 128 + 128)
                dx = xc - xy_row[0, j, :, half][None]
                dy = yc - xy_row[1, j, :, half][None]
                d = -(dx * dx) - dy * dy
                dist[st * step : st * step + step, half] = d.reshape(step, 128)
        for q in range(NW):
            for st in range(TB // step):
                sq = sq_col[q, pl.ds(row0 + st * step, step), :].reshape(step // 8, 8, 128)
                parts = []
                for c in range(2):
                    half = slice(c * 128, c * 128 + 128)
                    root = lax.rsqrt(sq + sq_row[q, j, :, half][None])
                    d = dist[st * step : st * step + step, half].reshape(step // 8, 8, 128)
                    parts.append((root * jnp.exp2(root * root * d)).reshape(step, 128).astype(BF16))
                kern_ref[t, q, st * step : st * step + step, :] = jnp.concatenate(parts, axis=1)
            times_tile(x_ref, y_ref, q, i, j, kern_ref[t, q], both)

    @pl.loop(0, NB)
    def _(t):
        tile(t, False)

    @pl.loop(NB, NT)
    def _(t):
        tile(t, True)

    send_rows(y_ref, scale_ref, amp_ref)
    for one in copies:
        one.wait()

    @pl.loop(0, TILES)
    def _(n):
        first = bins_ref[0, n * T]
        edge_ref[n] = first
        edge_ref[TILES + n] = bins_ref[0, n * T + T - 1] - first


def pull_kernel(g_ref, scale_ref, kern_ref, out_ref, x_ref, y_ref):
    for k in range(B // 128):
        a = g_ref[32 * k : 32 * k + 16, :].astype(F32)
        b = g_ref[32 * k + 16 : 32 * k + 32, :].astype(F32)
        take_vectors(a, b, k, x_ref, scale_ref)
    y_ref[...] = jnp.zeros_like(y_ref)

    def tile(t, both):
        i, j = tile_place(t)
        for q in range(NW):
            times_tile(x_ref, y_ref, q, i, j, kern_ref[t, q], both)

    @pl.loop(0, NB)
    def _(t):
        tile(t, False)

    @pl.loop(NB, NT)
    def _(t):
        tile(t, True)

    send_rows(y_ref, scale_ref, out_ref)


def wave_rows(ref, sp):
    return jnp.concatenate([ref[pl.ds(q * SP + sp, G, stride=16), :] for q in range(NW)], axis=0)


def forward_kernel(edge_ref, seg_ref, amp_ref, psi_ref, out0, out1, out2, out3, rows_ref, table, acc):
    me = lax.axis_index("wave")

    def tiles(k, m):
        tile = ((me + k) & (NX - 1)) * (Q // T) + m * 2
        return [(u, half, tile + half * (HQ // T) + u) for u in range(2) for half in range(2)]

    rows_ref[...] = amp_ref[...].astype(F32)
    table[...] = jnp.zeros_like(table)
    for sp in range(SP):
        flipped = wave_rows(rows_ref, sp).T
        for s2 in range(2):
            table[pl.ds(sp + SP * s2, R, stride=S), :] = flipped[s2 * R : s2 * R + R]

    for k, out_ref in enumerate((out0, out1, out2, out3)):

        @pl.loop(0, 4)
        def _(m):
            places = tiles(k, m)

            def select(u, half, tile, first, start):
                window = table[pl.ds(pl.multiple_of(first * S, S), NWIN * S), :].astype(BF16)
                values = psi_ref[pl.ds(pl.multiple_of(tile * T, T), T), :]
                fields = lax.dot_general(
                    window, values, (((1,), (1,)), ((), ())), preferred_element_type=F32
                )
                seg = jnp.broadcast_to(seg_ref[0:1, pl.ds(pl.multiple_of(tile * T, T), T)], (S, T)) - first
                for g in range(NWIN):
                    start = jnp.where(seg == g, fields[g * S : g * S + S], start)
                return start

            spans = []
            for u, half, tile in places:
                first = edge_ref[tile]
                acc[u, half * S : half * S + S, :] = select(u, half, tile, first, jnp.zeros((S, T), F32))
                spans.append(edge_ref[TILES + tile])
            widest = jnp.maximum(jnp.maximum(spans[0], spans[1]), jnp.maximum(spans[2], spans[3]))

            @pl.when(widest >= NWIN)
            def _():
                for (u, half, tile), span in zip(places, spans):
                    first = edge_ref[tile]

                    @pl.loop(1, span // NWIN + 1)
                    def _(w):
                        old = acc[u, half * S : half * S + S, :]
                        acc[u, half * S : half * S + S, :] = select(u, half, tile, first + w * NWIN, old)

            for u in range(2):
                out_ref[:, pl.ds(pl.multiple_of(m * 1024 + u * T, T), T)] = acc[u].astype(BF16)


def weight_kernel(a_ref, b_ref, c_ref, d_ref, out_ref):
    field = (a_ref[...].astype(F32) + b_ref[...].astype(F32)) + (c_ref[...].astype(F32) + d_ref[...].astype(F32))
    out_ref[...] = (-2.0 / S * field / (1.0 + field * field)).astype(BF16)


def backward_kernel(edge_ref, w0_ref, w1_ref, w2_ref, w3_ref, seg_ref, amp_ref, norm_ref, psi_ref, out_ref, rows_ref, sums):
    me = lax.axis_index("wave")

    def tiles(k, m):
        tile = ((me - k) & (NX - 1)) * (Q // T) + m * 2
        return [(u, half, tile + half * (HQ // T) + u) for u in range(2) for half in range(2)]

    sums[...] = jnp.zeros_like(sums)
    for k, w_ref in enumerate((w0_ref, w1_ref, w2_ref, w3_ref)):

        @pl.loop(0, 4)
        def _(m):
            places = tiles(k, m)

            def add(u, half, tile, first):
                weight = w_ref[:, pl.ds(pl.multiple_of(m * 1024 + u * T, T), T)].astype(F32)
                weight = weight[half * S : half * S + S]
                values = psi_ref[pl.ds(pl.multiple_of(tile * T, T), T), :]
                seg = jnp.broadcast_to(seg_ref[0:1, pl.ds(pl.multiple_of(tile * T, T), T)], (S, T)) - first
                spread = jnp.concatenate([jnp.where(seg == g, weight, 0.0) for g in range(NWIN)], axis=0)
                added = jnp.dot(spread.astype(BF16), values, preferred_element_type=F32)
                sums[pl.ds(pl.multiple_of(first * S, S), NWIN * S), :] += added

            spans = []
            for u, half, tile in places:
                first = edge_ref[tile]
                add(u, half, tile, first)
                spans.append(edge_ref[TILES + tile])
            widest = jnp.maximum(jnp.maximum(spans[0], spans[1]), jnp.maximum(spans[2], spans[3]))

            @pl.when(widest >= NWIN)
            def _():
                for (u, half, tile), span in zip(places, spans):
                    first = edge_ref[tile]

                    @pl.loop(1, span // NWIN + 1)
                    def _(w):
                        add(u, half, tile, first + w * NWIN)

    rows_ref[...] = amp_ref[...].astype(F32)
    norm = (jnp.concatenate([norm_ref[...]] * 2, axis=0) * (2.0 / S)).T
    for sp in range(SP):
        pair = [sums[pl.ds(sp + SP * s2, R, stride=S), :] for s2 in range(2)]
        flipped = jnp.concatenate(pair, axis=0).T
        for q in range(NW):
            where = pl.ds(q * SP + sp, G, stride=16)
            rows_ref[where, :] = rows_ref[where, :] * norm[q * G : q * G + G] + flipped[q * G : q * G + G]
    out_ref[...] = rows_ref[...].astype(BF16)


def unpack_kernel(r_ref, lat_ref, out_ref):
    for sp in range(SP):
        flipped = wave_rows(r_ref, sp).T
        for s2 in range(2):
            s = sp + SP * s2
            out_ref[s] = flipped[s2 * R : s2 * R + R] + lat_ref[s].astype(F32)


def exchange(x, rows):
    y = lax.all_to_all(x.reshape(G, rows, 128), "event", 0, 0)
    return y.reshape(G * rows, 128)


def shift(x, k):
    return lax.ppermute(x, "wave", [(i, (i + k) % NX) for i in range(NX)])


def vmem(shape, dtype=BF16):
    return pltpu.VMEM(shape, dtype)


def call(kernel, name, out_shape, args, scratch=(), spaces=None, out_specs=None, mib=8):
    spaces = spaces or "v" * len(args)
    kept = {"v": pltpu.VMEM, "h": pltpu.HBM}
    args = [pltpu.with_memory_space_constraint(a, kept[c]) if c in kept else a for a, c in zip(args, spaces)]
    return pl.pallas_call(
        kernel,
        out_shape=out_shape,
        in_specs=[{"v": VMEM, "h": ANY, "s": SMEM}[c] for c in spaces],
        out_specs=out_specs or jax.tree.map(lambda _: VMEM, out_shape),
        scratch_shapes=scratch,
        compiler_params=pltpu.CompilerParams(vmem_limit_bytes=mib * 1024 * 1024),
        name=name,
    )(*args)


def shards(latent, basis, event_bin, length, amplitude_scale, yield_norm, bin_coords):
    latent = latent.transpose(0, 2, 1)
    packed, coords, lat_kept = call(
        pack_kernel,
        "pack",
        (vmem((G * IN_ROWS, 128)), vmem((2, B), F32), vmem((S, R, WL))),
        (latent, length.T, amplitude_scale.T, bin_coords),
        [
            vmem((R, WL), F32),
            vmem((R, WL), F32),
            vmem((G * IN_ROWS, 128), F32),
            pltpu.SemaphoreType.DMA((4,)),
        ],
        "hhhh",
    )
    kern, amp_out, scale, psi, seg, norm, edges = call(
        gen_kernel,
        "gen",
        (
            vmem((NT, NW, TB, TB)),
            vmem((G * 16, 128)),
            vmem((8, B), F32),
            vmem((E, WL)),
            vmem((1, E), jnp.int32),
            vmem((R, WL), F32),
            jax.ShapeDtypeStruct((2 * TILES,), jnp.int32),
        ),
        (exchange(packed, IN_ROWS), coords, basis, event_bin, yield_norm.T),
        [
            vmem((G * IN_ROWS, 128), F32),
            vmem((2, 8, B), F32),
            vmem((NW, NB, 16, TB)),
            vmem((NW, NB, 16, TB), F32),
            vmem((NW, NB, 8, TB), F32),
            vmem((NW, B, 128), F32),
            vmem((2, NB, 8, TB), F32),
            vmem((2, B, 128), F32),
            vmem((TB, TB), F32),
            pltpu.SMEM((1, E), jnp.int32),
            pltpu.SemaphoreType.DMA((4,)),
        ],
        "vvhhh",
        (VMEM,) * 6 + (SMEM,),
        mib=12,
    )
    amp_in = exchange(amp_out, 16)
    fields = call(
        forward_kernel,
        "forward",
        [vmem((2 * S, HQ))] * NX,
        (edges, seg, amp_in, psi),
        [
            vmem((G * 16, 128), F32),
            vmem(((R + NWIN) * S, 128), F32),
            vmem((2, 2 * S, T), F32),
        ],
        "svvv",
    )
    others = [shift(fields[k], k) for k in range(1, NX)]
    weight = call(weight_kernel, "weight", vmem((2 * S, HQ)), (fields[0], *others))
    weights = [weight] + [shift(weight, k) for k in range(1, NX)]
    grad_out = call(
        backward_kernel,
        "backward",
        vmem((G * 16, 128)),
        (edges, *weights, seg, amp_in, norm, psi),
        [vmem((G * 16, 128), F32), vmem(((R + NWIN) * S, 128), F32)],
        "svvvvvvvv",
    )
    pulled = call(
        pull_kernel,
        "pull",
        vmem((G * 16, 128), F32),
        (exchange(grad_out, 16), scale, kern),
        [vmem((NW, NB, 16, TB)), vmem((NW, NB, 16, TB), F32)],
    )
    out = call(
        unpack_kernel,
        "unpack",
        jax.ShapeDtypeStruct((S, R, WL), F32),
        (exchange(pulled, 16), lat_kept),
    )
    return out.transpose(0, 2, 1)


def solution(mesh):
    placed = (
        P(None, "wave", "event"),
        P("event", "wave"),
        P("event", None),
        P("wave", "event"),
        P("wave", "event"),
        P("wave", "event"),
        P(),
    )
    return jax.shard_map(
        shards, mesh=mesh, in_specs=placed, out_specs=P(None, "wave", "event"), check_vma=False
    )
```

time: 148 us -> 119 us (0.80)
  Pallas kernels: 60.4 us -> 44.2 us
  local copies, waits for them, and re-layouts: 10.7 us -> 0 us
  blocking collectives: 47.8 us -> 53.6 us
  starting transfers between devices: 12.8 us -> 7.89 us
  waiting for transfers between devices: 15.6 us -> 12.8 us
    pallas_call x7, Pallas kernels: 60.4 us -> 44.2 us  [call(): pl.pallas_call(kernel, out_shape=out_shape, in_specs=[{'v': VMEM, 'h': AN...]
    unnamed x18 -> x0, local copies, waits for them, and re-layouts: 8.82 us -> none
    all_to_all x1 -> x0, waiting for transfers between devices: 7.74 us -> none  [exchange(): y = lax.all_to_all(x.reshape(G, rows, 128), 'event', 0, 0)]
    all_to_all x3 -> x4, blocking collectives: 47.8 us -> 53.6 us  [exchange(): y = lax.all_to_all(x.reshape(G, rows, 128), 'event', 0, 0)]
    ppermute x6, waiting for transfers between devices: 7.82 us -> 12.8 us  [shift(): return lax.ppermute(x, 'wave', [(i, (i + k) % NX) for i in range(NX)])]
    all_to_all x1 -> x0, starting transfers between devices: 3.87 us -> none  [exchange(): y = lax.all_to_all(x.reshape(G, rows, 128), 'event', 0, 0)]
    pallas_call x1 -> x0, local copies, waits for them, and re-layouts: 1.93 us -> none  [shards(): pl.pallas_call(unpack_kernel, out_shape=struct((S, WL, R), F32), in_specs...]
  transfers between devices with their start and end apart: 7 -> 6, of which waited for: 5 -> 5; matrix products, arithmetic and copies ran while one was open for 1% -> 0% of each run, Pallas kernels for 0% -> 0%
where the time goes in v2:
time: 119 us
  blocking collectives  53.6 us (45%)
  Pallas kernels  44.2 us (37%)
  waiting for transfers between devices  12.8 us (11%)
  starting transfers between devices  7.89 us (7%)
    all_to_all x4, blocking collectives, exchange(): y = lax.all_to_all(x.reshape(G, rows, 128), 'event', 0, 0)  53.6 us
    pallas_call x7, Pallas kernels, call(): pl.pallas_call(kernel, out_shape=out_shape, in_specs=[{'v': VMEM, 'h': AN...  44.2 us
    ppermute x6, waiting for transfers between devices, shift(): return lax.ppermute(x, 'wave', [(i, (i + k) % NX) for i in range(NX)])  12.8 us
    ppermute x6, starting transfers between devices, shift(): return lax.ppermute(x, 'wave', [(i, (i + k) % NX) for i in range(NX)])  7.89 us
  transfers between devices with their start and end apart: 6, of which 5 were waited for; matrix products, arithmetic and copies ran while one was open for 0% of the time, Pallas kernels for 0%

profile of v2, /device:TPU:1, one launch (start us, length us, event | category | flops | bytes accessed | tf_op | source)
XLA Modules:
  0.0 118.6 jit_solution(7934540719119894017)
XLA Ops:
  0.0 1.2 pack.1
  1.2 17.7 %all_to_all.20 = bf16[32,24,128]{2,1,0:T(8,128)(2,1)S(1)} all-to-all(bf16[32,24,128]{2,1,0:T(8,128)(2,1)S(1)} %bitcast.20), channel_id=1, replica_groups=mesh['wave'=4,'event'=32] {'event'}, dimensions={0} | all-to-all | bytes 393216 | tf_op jit(solution)/shard_map/all_to_all | solution.py:342
  18.8 21.0 %gen.1 = (bf16[36,4,256,256]{3,2,1,0:T(8,128)(2,1)S(1)}, bf16[512,128]{1,0:T(8,128)(2,1)S(1)}, f32[8,2048]{1,0:T(8,128)S(1)}, bf16[32768,128]{1,0:T(8,128)(2,1)S...) custom-call(bf16[768,128]{1,0:T(8,128)(2,1)S(1)} %bitcast.17, ...), custom_call_target="tpu_custom_call" | custom-call | tf_op jit(solution)/shard_map/gen/pallas_call | solution.py:358
  39.9 11.2 %all_to_all.21 = bf16[32,16,128]{2,1,0:T(8,128)(2,1)S(1)} all-to-all(bf16[32,16,128]{2,1,0:T(8,128)(2,1)S(1)} %bitcast.21), channel_id=1, replica_groups=mesh['wave'=4,'event'=32] {'event'}, dimensions={0} | all-to-all | bytes 262144 | tf_op jit(solution)/shard_map/all_to_all | solution.py:342
  51.1 5.6 %forward.1 = (bf16[16,4096]{1,0:T(8,128)(2,1)S(1)}, bf16[16,4096]{1,0:T(8,128)(2,1)S(1)}, bf16[16,4096]{1,0:T(8,128)(2,1)S(1)}, bf16[16,4096]{1,0:T(8,128)(2,1)S(1)}) custom-call(s32[128]{0:T(128)S(1)} %get-tuple-element.21.edge_ref, s32[1,32768]{1,0:T(1,128)S(1)} %get-tuple-element.22.seg_ref, bf16[512,128]{1,0:T(8,128)(2,1)S(1)} %bitcast.13, ...), custom_call_target="tpu_custom_call" | custom-call | tf_op jit(solution)/shard_map/forward/pallas_call | solution.py:358
  56.7 1.3 %collective-permute-start = (bf16[16,4096]{1,0:T(8,128)(2,1)S(1)}, bf16[16,4096]{1,0:T(8,128)(2,1)S(1)}, u32[]{:S(2)}, u32[]{:S(2)}) collective-permute-start(bf16[16,4096]{1,0:T(8,128)(2,1)S(1)} %get-tuple-element.26), channel_id=1, source_target_pairs={{0,32},{32,64},{64,96},{96,0},{1,33},{33,65},{65,97},{97,1},{2,34}... | collective-permute-start | bytes 393224 | tf_op jit(solution)/shard_map/ppermute | solution.py:347
  58.0 2.4 %collective-permute-start.1 = (bf16[16,4096]{1,0:T(8,128)(2,1)S(1)}, bf16[16,4096]{1,0:T(8,128)(2,1)S(1)}, u32[]{:S(2)}, u32[]{:S(2)}) collective-permute-start(bf16[16,4096]{1,0:T(8,128)(2,1)S(1)} %get-tuple-element.27), channel_id=1, source_target_pairs={{0,64},{32,96},{64,0},{96,32},{1,65},{33,97},{65,1},{97,33},{2,66}... | collective-permute-start | bytes 393224 | tf_op jit(solution)/shard_map/ppermute | solution.py:347
  60.4 1.1 collective-permute-start.2
  61.6 1.1 collective-permute-done.b_ref
  62.6 3.8 %collective-permute-done.1.c_ref = bf16[16,4096]{1,0:T(8,128)(2,1)S(1)} collective-permute-done((bf16[16,4096]{1,0:T(8,128)(2,1)S(1)}, bf16[16,4096]{1,0:T(8,128)(2,1)S(1)}, u32[]{:S(2)}, u32[]{:S(2)}) %collective-permute-start.1) | collective-permute-done | bytes 131104 | tf_op jit(solution)/shard_map/ppermute | solution.py:347
  66.4 0.0 collective-permute-done.2.d_ref
  66.5 0.1 weight.1.w0_ref
  66.6 2.1 %collective-permute-start.5 = (bf16[16,4096]{1,0:T(8,128)(2,1)S(1)}, bf16[16,4096]{1,0:T(8,128)(2,1)S(1)}, u32[]{:S(2)}, u32[]{:S(2)}) collective-permute-start(bf16[16,4096]{1,0:T(8,128)(2,1)S(1)} %weight.1.w0_ref), channel_id=1, source_target_pairs={{0,96},{32,0},{64,32},{96,64},{1,97},{33,1},{65,33},{97,65},{2,98}... | collective-permute-start | bytes 393224 | tf_op jit(solution)/shard_map/ppermute | solution.py:347
  68.7 0.8 collective-permute-start.4
  69.5 0.1 collective-permute-start.3
  69.6 2.2 %collective-permute-done.5.w3_ref = bf16[16,4096]{1,0:T(8,128)(2,1)S(1)} collective-permute-done((bf16[16,4096]{1,0:T(8,128)(2,1)S(1)}, bf16[16,4096]{1,0:T(8,128)(2,1)S(1)}, u32[]{:S(2)}, u32[]{:S(2)}) %collective-permute-start.5) | collective-permute-done | bytes 131104 | tf_op jit(solution)/shard_map/ppermute | solution.py:347
  71.8 2.3 %collective-permute-done.4.w2_ref = bf16[16,4096]{1,0:T(8,128)(2,1)S(1)} collective-permute-done((bf16[16,4096]{1,0:T(8,128)(2,1)S(1)}, bf16[16,4096]{1,0:T(8,128)(2,1)S(1)}, u32[]{:S(2)}, u32[]{:S(2)}) %collective-permute-start.4) | collective-permute-done | bytes 131104 | tf_op jit(solution)/shard_map/ppermute | solution.py:347
  74.1 3.4 %collective-permute-done.3.w1_ref = bf16[16,4096]{1,0:T(8,128)(2,1)S(1)} collective-permute-done((bf16[16,4096]{1,0:T(8,128)(2,1)S(1)}, bf16[16,4096]{1,0:T(8,128)(2,1)S(1)}, u32[]{:S(2)}, u32[]{:S(2)}) %collective-permute-start.3) | collective-permute-done | bytes 131104 | tf_op jit(solution)/shard_map/ppermute | solution.py:347
  77.5 4.5 %backward.1 = bf16[512,128]{1,0:T(8,128)(2,1)S(1)} custom-call(s32[128]{0:T(128)S(1)} %get-tuple-element.21.edge_ref, bf16[16,4096]{1,0:T(8,128)(2,1)S(1)} %weight.1.w0_ref, bf16[16,4096]{1,0:T(8,128)(2,1)S(1)} %collective-permute-done.3.w1_ref, bf16[16,4096]{1,0:T(8,128)(2,1)S(1)} %collective-permute-done.4.w2_ref, ...), custom_call_target="tpu_custom_call" | custom-call | tf_op jit(solution)/shard_map/backward/pallas_call | solution.py:358
  82.0 12.2 %all_to_all.22 = bf16[32,16,128]{2,1,0:T(8,128)(2,1)S(1)} all-to-all(bf16[32,16,128]{2,1,0:T(8,128)(2,1)S(1)} %bitcast.18), channel_id=1, replica_groups=mesh['wave'=4,'event'=32] {'event'}, dimensions={0} | all-to-all | bytes 262144 | tf_op jit(solution)/shard_map/all_to_all | solution.py:342
  94.2 11.0 %pull.1 = f32[512,128]{1,0:T(8,128)S(1)} custom-call(bf16[512,128]{1,0:T(8,128)(2,1)S(1)} %bitcast.19, f32[8,2048]{1,0:T(8,128)S(1)} %get-tuple-element.30.scale_ref, bf16[36,4,256,256]{3,2,1,0:T(8,128)(2,1)S(1)} %get-tuple-element.31.kern_ref), custom_call_target="tpu_custom_call" | custom-call | tf_op jit(solution)/shard_map/pull/pallas_call | solution.py:358
  105.2 12.5 %all_to_all.23 = f32[32,16,128]{2,1,0:T(8,128)S(1)} all-to-all(f32[32,16,128]{2,1,0:T(8,128)S(1)} %bitcast.15), channel_id=1, replica_groups=mesh['wave'=4,'event'=32] {'event'}, dimensions={0} | all-to-all | bytes 524288 | tf_op jit(solution)/shard_map/all_to_all | solution.py:342
  117.7 0.8 unpack.1
Async XLA Ops:
  56.7 5.9 %collective-permute-start = (bf16[16,4096]{1,0:T(8,128)(2,1)S(1)}, bf16[16,4096]{1,0:T(8,128)(2,1)S(1)}, u32[]{:S(2)}, u32[]{:S(2)}) collective-permute-start(bf16[16,4096]{1,0:T(8,128)(2,1)S(1)} %get-tuple-element.26), channel_id=1, source_target_pairs={{0,32},{32,64},{64,96},{96,0},{1,33},{33,65},{65,97},{97,1},{2,34}... | collective-permute-start | bytes 393224 | tf_op jit(solution)/shard_map/ppermute | solution.py:347
  58.0 8.4 %collective-permute-start.1 = (bf16[16,4096]{1,0:T(8,128)(2,1)S(1)}, bf16[16,4096]{1,0:T(8,128)(2,1)S(1)}, u32[]{:S(2)}, u32[]{:S(2)}) collective-permute-start(bf16[16,4096]{1,0:T(8,128)(2,1)S(1)} %get-tuple-element.27), channel_id=1, source_target_pairs={{0,64},{32,96},{64,0},{96,32},{1,65},{33,97},{65,1},{97,33},{2,66}... | collective-permute-start | bytes 393224 | tf_op jit(solution)/shard_map/ppermute | solution.py:347
  60.4 6.0 %collective-permute-start.2 = (bf16[16,4096]{1,0:T(8,128)(2,1)S(1)}, bf16[16,4096]{1,0:T(8,128)(2,1)S(1)}, u32[]{:S(2)}, u32[]{:S(2)}) collective-permute-start(bf16[16,4096]{1,0:T(8,128)(2,1)S(1)} %get-tuple-element.28), channel_id=1, source_target_pairs={{0,96},{32,0},{64,32},{96,64},{1,97},{33,1},{65,33},{97,65},{2,98}... | collective-permute-start | bytes 393224 | tf_op jit(solution)/shard_map/ppermute | solution.py:347
  66.6 5.2 %collective-permute-start.5 = (bf16[16,4096]{1,0:T(8,128)(2,1)S(1)}, bf16[16,4096]{1,0:T(8,128)(2,1)S(1)}, u32[]{:S(2)}, u32[]{:S(2)}) collective-permute-start(bf16[16,4096]{1,0:T(8,128)(2,1)S(1)} %weight.1.w0_ref), channel_id=1, source_target_pairs={{0,96},{32,0},{64,32},{96,64},{1,97},{33,1},{65,33},{97,65},{2,98}... | collective-permute-start | bytes 393224 | tf_op jit(solution)/shard_map/ppermute | solution.py:347
  68.7 5.4 %collective-permute-start.4 = (bf16[16,4096]{1,0:T(8,128)(2,1)S(1)}, bf16[16,4096]{1,0:T(8,128)(2,1)S(1)}, u32[]{:S(2)}, u32[]{:S(2)}) collective-permute-start(bf16[16,4096]{1,0:T(8,128)(2,1)S(1)} %weight.1.w0_ref), channel_id=1, source_target_pairs={{0,64},{32,96},{64,0},{96,32},{1,65},{33,97},{65,1},{97,33},{2,66}... | collective-permute-start | bytes 393224 | tf_op jit(solution)/shard_map/ppermute | solution.py:347
  69.5 8.0 %collective-permute-start.3 = (bf16[16,4096]{1,0:T(8,128)(2,1)S(1)}, bf16[16,4096]{1,0:T(8,128)(2,1)S(1)}, u32[]{:S(2)}, u32[]{:S(2)}) collective-permute-start(bf16[16,4096]{1,0:T(8,128)(2,1)S(1)} %weight.1.w0_ref), channel_id=1, source_target_pairs={{0,32},{32,64},{64,96},{96,0},{1,33},{33,65},{65,97},{97,1},{2,34}... | collective-permute-start | bytes 393224 | tf_op jit(solution)/shard_map/ppermute | solution.py:347

commit v3 on v2

--- a/solution.py
+++ b/solution.py
@@ -1,3 +1,4 @@
+import functools
 import math
 
 import jax
@@ -177,11 +178,11 @@
                 kern_ref[t, q, st * step : st * step + step, :] = jnp.concatenate(parts, axis=1)
             times_tile(x_ref, y_ref, q, i, j, kern_ref[t, q], both)
 
-    @pl.loop(0, NB)
+    @pl.loop(0, NB, unroll=8)
     def _(t):
         tile(t, False)
 
-    @pl.loop(NB, NT)
+    @pl.loop(NB, NT, unroll=7)
     def _(t):
         tile(t, True)
 
@@ -189,11 +190,15 @@
     for one in copies:
         one.wait()
 
-    @pl.loop(0, TILES)
-    def _(n):
-        first = bins_ref[0, n * T]
-        edge_ref[n] = first
-        edge_ref[TILES + n] = bins_ref[0, n * T + T - 1] - first
+    for quarter in range(NX):
+        widest = jnp.int32(0)
+        for n in range(quarter * TILES // NX, (quarter + 1) * TILES // NX):
+            first = bins_ref[0, n * T]
+            span = bins_ref[0, n * T + T - 1] - first
+            edge_ref[n] = first
+            edge_ref[TILES + n] = span
+            widest = jnp.maximum(widest, span)
+        edge_ref[2 * TILES + quarter] = widest
 
 
 def pull_kernel(g_ref, scale_ref, kern_ref, out_ref, x_ref, y_ref):
@@ -208,11 +213,11 @@
         for q in range(NW):
             times_tile(x_ref, y_ref, q, i, j, kern_ref[t, q], both)
 
-    @pl.loop(0, NB)
+    @pl.loop(0, NB, unroll=8)
     def _(t):
         tile(t, False)
 
-    @pl.loop(NB, NT)
+    @pl.loop(NB, NT, unroll=7)
     def _(t):
         tile(t, True)
 
@@ -223,56 +228,65 @@
     return jnp.concatenate([ref[pl.ds(q * SP + sp, G, stride=16), :] for q in range(NW)], axis=0)
 
 
-def forward_kernel(edge_ref, seg_ref, amp_ref, psi_ref, out0, out1, out2, out3, rows_ref, table, acc):
-    me = lax.axis_index("wave")
-
-    def tiles(k, m):
-        tile = ((me + k) & (NX - 1)) * (Q // T) + m * 2
-        return [(u, half, tile + half * (HQ // T) + u) for u in range(2) for half in range(2)]
-
+def table_kernel(amp_ref, table_ref, rows_ref):
     rows_ref[...] = amp_ref[...].astype(F32)
-    table[...] = jnp.zeros_like(table)
+    table_ref[R * S :, :] = jnp.zeros((NWIN * S, WL), F32)
     for sp in range(SP):
         flipped = wave_rows(rows_ref, sp).T
         for s2 in range(2):
-            table[pl.ds(sp + SP * s2, R, stride=S), :] = flipped[s2 * R : s2 * R + R]
-
-    for k, out_ref in enumerate((out0, out1, out2, out3)):
-
-        @pl.loop(0, 4)
+            table_ref[pl.ds(sp + SP * s2, R, stride=S), :] = flipped[s2 * R : s2 * R + R]
+
+
+def quarter_tiles(quarter, m):
+    tile = quarter * (Q // T) + m
+    return tile, tile + HQ // T
+
+
+def tile_bins(seg_ref, tile, first):
+    return jnp.broadcast_to(seg_ref[0:1, pl.ds(pl.multiple_of(tile * T, T), T)], (S, T)) - first
+
+
+def tile_basis(psi_ref, tile):
+    return psi_ref[pl.ds(pl.multiple_of(tile * T, T), T), :]
+
+
+def forward_kernel(k, edge_ref, seg_ref, table_ref, psi_ref, out_ref):
+    quarter = (lax.axis_index("wave") + k) & (NX - 1)
+
+    def select(tile, first, start):
+        window = table_ref[pl.ds(pl.multiple_of(first * S, S), NWIN * S), :].astype(BF16)
+        fields = lax.dot_general(
+            window, tile_basis(psi_ref, tile), (((1,), (1,)), ((), ())), preferred_element_type=F32
+        )
+        seg = tile_bins(seg_ref, tile, first)
+        for g in range(NWIN):
+            start = jnp.where(seg == g, fields[g * S : g * S + S], start)
+        return start
+
+    def put(m, parts):
+        out_ref[:, pl.ds(pl.multiple_of(m * T, T), T)] = jnp.concatenate(parts, axis=0).astype(BF16)
+
+    zero = jnp.zeros((S, T), F32)
+
+    for m in range(HQ // T):
+        put(m, [select(tile, edge_ref[tile], zero) for tile in quarter_tiles(quarter, m)])
+
+    @pl.when(edge_ref[2 * TILES + quarter] >= NWIN)
+    def _():
+        @pl.loop(0, HQ // T)
         def _(m):
-            places = tiles(k, m)
-
-            def select(u, half, tile, first, start):
-                window = table[pl.ds(pl.multiple_of(first * S, S), NWIN * S), :].astype(BF16)
-                values = psi_ref[pl.ds(pl.multiple_of(tile * T, T), T), :]
-                fields = lax.dot_general(
-                    window, values, (((1,), (1,)), ((), ())), preferred_element_type=F32
-                )
-                seg = jnp.broadcast_to(seg_ref[0:1, pl.ds(pl.multiple_of(tile * T, T), T)], (S, T)) - first
-                for g in range(NWIN):
-                    start = jnp.where(seg == g, fields[g * S : g * S + S], start)
-                return start
-
-            spans = []
-            for u, half, tile in places:
-                first = edge_ref[tile]
-                acc[u, half * S : half * S + S, :] = select(u, half, tile, first, jnp.zeros((S, T), F32))
-                spans.append(edge_ref[TILES + tile])
-            widest = jnp.maximum(jnp.maximum(spans[0], spans[1]), jnp.maximum(spans[2], spans[3]))
-
-            @pl.when(widest >= NWIN)
-            def _():
-                for (u, half, tile), span in zip(places, spans):
-                    first = edge_ref[tile]
-
-                    @pl.loop(1, span // NWIN + 1)
-                    def _(w):
-                        old = acc[u, half * S : half * S + S, :]
-                        acc[u, half * S : half * S + S, :] = select(u, half, tile, first + w * NWIN, old)
-
-            for u in range(2):
-                out_ref[:, pl.ds(pl.multiple_of(m * 1024 + u * T, T), T)] = acc[u].astype(BF16)
+            put(
+                m,
+                [
+                    lax.fori_loop(
+                        0,
+                        edge_ref[TILES + tile] // NWIN + 1,
+                        lambda w, acc: select(tile, edge_ref[tile] + w * NWIN, acc),
+                        zero,
+                    )
+                    for tile in quarter_tiles(quarter, m)
+                ],
+            )
 
 
 def weight_kernel(a_ref, b_ref, c_ref, d_ref, out_ref):
@@ -280,45 +294,40 @@
     out_ref[...] = (-2.0 / S * field / (1.0 + field * field)).astype(BF16)
 
 
-def backward_kernel(edge_ref, w0_ref, w1_ref, w2_ref, w3_ref, seg_ref, amp_ref, norm_ref, psi_ref, out_ref, rows_ref, sums):
-    me = lax.axis_index("wave")
-
-    def tiles(k, m):
-        tile = ((me - k) & (NX - 1)) * (Q // T) + m * 2
-        return [(u, half, tile + half * (HQ // T) + u) for u in range(2) for half in range(2)]
-
-    sums[...] = jnp.zeros_like(sums)
-    for k, w_ref in enumerate((w0_ref, w1_ref, w2_ref, w3_ref)):
-
-        @pl.loop(0, 4)
+def add_quarter(k, edge_ref, w_ref, seg_ref, psi_ref, sums):
+    quarter = (lax.axis_index("wave") - k) & (NX - 1)
+
+    def add(m, half, tile, first):
+        weight = w_ref[:, pl.ds(pl.multiple_of(m * T, T), T)].astype(F32)[half * S : half * S + S]
+        seg = tile_bins(seg_ref, tile, first)
+        spread = jnp.concatenate([jnp.where(seg == g, weight, 0.0) for g in range(NWIN)], axis=0)
+        added = jnp.dot(spread.astype(BF16), tile_basis(psi_ref, tile), preferred_element_type=F32)
+        sums[pl.ds(pl.multiple_of(first * S, S), NWIN * S), :] += added
+
+    for m in range(HQ // T):
+        for half, tile in enumerate(quarter_tiles(quarter, m)):
+            add(m, half, tile, edge_ref[tile])
+
+    @pl.when(edge_ref[2 * TILES + quarter] >= NWIN)
+    def _():
+        @pl.loop(0, HQ // T)
         def _(m):
-            places = tiles(k, m)
-
-            def add(u, half, tile, first):
-                weight = w_ref[:, pl.ds(pl.multiple_of(m * 1024 + u * T, T), T)].astype(F32)
-                weight = weight[half * S : half * S + S]
-                values = psi_ref[pl.ds(pl.multiple_of(tile * T, T), T), :]
-                seg = jnp.broadcast_to(seg_ref[0:1, pl.ds(pl.multiple_of(tile * T, T), T)], (S, T)) - first
-                spread = jnp.concatenate([jnp.where(seg == g, weight, 0.0) for g in range(NWIN)], axis=0)
-                added = jnp.dot(spread.astype(BF16), values, preferred_element_type=F32)
-                sums[pl.ds(pl.multiple_of(first * S, S), NWIN * S), :] += added
-
-            spans = []
-            for u, half, tile in places:
-                first = edge_ref[tile]
-                add(u, half, tile, first)
-                spans.append(edge_ref[TILES + tile])
-            widest = jnp.maximum(jnp.maximum(spans[0], spans[1]), jnp.maximum(spans[2], spans[3]))
-
-            @pl.when(widest >= NWIN)
-            def _():
-                for (u, half, tile), span in zip(places, spans):
-                    first = edge_ref[tile]
-
-                    @pl.loop(1, span // NWIN + 1)
-                    def _(w):
-                        add(u, half, tile, first + w * NWIN)
-
+            for half, tile in enumerate(quarter_tiles(quarter, m)):
+
+                @pl.loop(1, edge_ref[TILES + tile] // NWIN + 1)
+                def _(w):
+                    add(m, half, tile, edge_ref[tile] + w * NWIN)
+
+
+def backward_first_kernel(edge_ref, w0_ref, seg_ref, psi_ref, sums_ref):
+    sums_ref[...] = jnp.zeros_like(sums_ref)
+    add_quarter(0, edge_ref, w0_ref, seg_ref, psi_ref, sums_ref)
+
+
+def backward_kernel(edge_ref, w1_ref, w2_ref, w3_ref, seg_ref, psi_ref, begun_ref, amp_ref, norm_ref, out_ref, rows_ref, sums):
+    sums[...] = begun_ref[...]
+    for k, w_ref in enumerate((w1_ref, w2_ref, w3_ref)):
+        add_quarter(k + 1, edge_ref, w_ref, seg_ref, psi_ref, sums)
     rows_ref[...] = amp_ref[...].astype(F32)
     norm = (jnp.concatenate([norm_ref[...]] * 2, axis=0) * (2.0 / S)).T
     for sp in range(SP):
@@ -391,7 +400,7 @@
             vmem((E, WL)),
             vmem((1, E), jnp.int32),
             vmem((R, WL), F32),
-            jax.ShapeDtypeStruct((2 * TILES,), jnp.int32),
+            jax.ShapeDtypeStruct((2 * TILES + NX,), jnp.int32),
         ),
         (exchange(packed, IN_ROWS), coords, basis, event_bin, yield_norm.T),
         [
@@ -412,27 +421,26 @@
         mib=12,
     )
     amp_in = exchange(amp_out, 16)
-    fields = call(
-        forward_kernel,
-        "forward",
-        [vmem((2 * S, HQ))] * NX,
-        (edges, seg, amp_in, psi),
-        [
-            vmem((G * 16, 128), F32),
-            vmem(((R + NWIN) * S, 128), F32),
-            vmem((2, 2 * S, T), F32),
-        ],
-        "svvv",
-    )
-    others = [shift(fields[k], k) for k in range(1, NX)]
-    weight = call(weight_kernel, "weight", vmem((2 * S, HQ)), (fields[0], *others))
-    weights = [weight] + [shift(weight, k) for k in range(1, NX)]
+    bins = (R + NWIN) * S
+    table = call(table_kernel, "table", vmem((bins, WL), F32), (amp_in,), [vmem((G * 16, 128), F32)])
+
+    def forward(k):
+        return call(
+            functools.partial(forward_kernel, k), "forward", vmem((2 * S, HQ)), (edges, seg, table, psi), spaces="svvv"
+        )
+
+    others = [shift(forward(k), k) for k in (2, 1, 3)]
+    weight = call(weight_kernel, "weight", vmem((2 * S, HQ)), (forward(0), *others))
+    weights = [shift(weight, k) for k in range(1, NX)]
+    begun = call(
+        backward_first_kernel, "backward0", vmem((bins, WL), F32), (edges, weight, seg, psi), spaces="svvv"
+    )
     grad_out = call(
         backward_kernel,
         "backward",
         vmem((G * 16, 128)),
-        (edges, *weights, seg, amp_in, norm, psi),
-        [vmem((G * 16, 128), F32), vmem(((R + NWIN) * S, 128), F32)],
+        (edges, *weights, seg, psi, begun, amp_in, norm),
+        [vmem((G * 16, 128), F32), vmem((bins, WL), F32)],
         "svvvvvvvv",
     )
     pulled = call(

time: 119 us -> 104 us (0.87)
  Pallas kernels: 44.2 us -> 32.1 us
  waiting for transfers between devices: 12.8 us -> 9.42 us
    pallas_call x7 -> x12, Pallas kernels: 44.2 us -> 32.1 us  [call(): pl.pallas_call(kernel, out_shape=out_shape, in_specs=[{'v': VMEM, 'h': AN...]
    ppermute x6, waiting for transfers between devices: 12.8 us -> 9.42 us  [shift(): return lax.ppermute(x, 'wave', [(i, (i + k) % NX) for i in range(NX)])]
  transfers between devices with their start and end apart: 6 -> 6, of which waited for: 5 -> 4; matrix products, arithmetic and copies ran while one was open for 0% -> 0% of each run, Pallas kernels for 0% -> 2%
where the time goes in v3:
time: 104 us
  blocking collectives  53.5 us (51%)
  Pallas kernels  32.1 us (31%)
  waiting for transfers between devices  9.42 us (9%)
  starting transfers between devices  8.81 us (8%)
    all_to_all x4, blocking collectives, exchange(): y = lax.all_to_all(x.reshape(G, rows, 128), 'event', 0, 0)  53.5 us
    pallas_call x12, Pallas kernels, call(): pl.pallas_call(kernel, out_shape=out_shape, in_specs=[{'v': VMEM, 'h': AN...  32.1 us
    ppermute x6, waiting for transfers between devices, shift(): return lax.ppermute(x, 'wave', [(i, (i + k) % NX) for i in range(NX)])  9.42 us
    ppermute x6, starting transfers between devices, shift(): return lax.ppermute(x, 'wave', [(i, (i + k) % NX) for i in range(NX)])  8.81 us
  transfers between devices with their start and end apart: 6, of which 4 were waited for; matrix products, arithmetic and copies ran while one was open for 0% of the time, Pallas kernels for 2%

profile of v3, /device:TPU:1, one launch (start us, length us, event | category | flops | bytes accessed | tf_op | source)
XLA Modules:
  0.0 103.9 jit_solution(6667991974401556372)
XLA Ops:
  0.0 1.2 %pack.1 = (bf16[768,128]{1,0:T(8,128)(2,1)S(1)}, f32[2,2048]{1,0:T(2,128)S(1)}, bf16[8,64,128]{2,1,0:T(8,128)(2,1)S(1)}) custom-call(bf16[8,64,128]{2,1,0:T(8,128)(2,1)} %bitcast.22, f32[64,128]{1,0:T(8,128)} %bitcast.24, f32[64,128]{1,0:T(8,128)} %bitcast.25, f32[2,2048]{1,0:T(2,128)} %xy_hbm.1), custom_call_target="tpu_custom_call" | custom-call | tf_op jit(solution)/shard_map/pack/pallas_call | solution.py:367
  1.2 17.7 %all_to_all.20 = bf16[32,24,128]{2,1,0:T(8,128)(2,1)S(1)} all-to-all(bf16[32,24,128]{2,1,0:T(8,128)(2,1)S(1)} %bitcast.20), channel_id=1, replica_groups=mesh['wave'=4,'event'=32] {'event'}, dimensions={0} | all-to-all | bytes 393216 | tf_op jit(solution)/shard_map/all_to_all | solution.py:351
  18.8 13.7 %gen.1 = (bf16[36,4,256,256]{3,2,1,0:T(8,128)(2,1)S(1)}, bf16[512,128]{1,0:T(8,128)(2,1)S(1)}, f32[8,2048]{1,0:T(8,128)S(1)}, bf16[32768,128]{1,0:T(8,128)(2,1)S...) custom-call(bf16[768,128]{1,0:T(8,128)(2,1)S(1)} %bitcast.17, ...), custom_call_target="tpu_custom_call" | custom-call | tf_op jit(solution)/shard_map/gen/pallas_call | solution.py:367
  32.5 11.2 %all_to_all.21 = bf16[32,16,128]{2,1,0:T(8,128)(2,1)S(1)} all-to-all(bf16[32,16,128]{2,1,0:T(8,128)(2,1)S(1)} %bitcast.21), channel_id=1, replica_groups=mesh['wave'=4,'event'=32] {'event'}, dimensions={0} | all-to-all | bytes 262144 | tf_op jit(solution)/shard_map/all_to_all | solution.py:351
  43.7 0.2 table.1.table_ref
  43.9 1.4 %forward.7 = bf16[16,4096]{1,0:T(8,128)(2,1)S(1)} custom-call(s32[132]{0:T(256)S(1)} %get-tuple-element.17.edge_ref, s32[1,32768]{1,0:T(1,128)S(1)} %get-tuple-element.18.seg_ref, f32[576,128]{1,0:T(8,128)S(1)} %table.1.table_ref, bf16[32768,128]{1,0:T(8,128)(2,1)S(1)} %get-tuple-element.20.psi_ref), custom_call_target="tpu_custom_call" | custom-call | tf_op jit(solution)/shard_map/forward/pallas_call | solution.py:367
  45.3 1.4 %forward.6 = bf16[16,4096]{1,0:T(8,128)(2,1)S(1)} custom-call(s32[132]{0:T(256)S(1)} %get-tuple-element.17.edge_ref, s32[1,32768]{1,0:T(1,128)S(1)} %get-tuple-element.18.seg_ref, f32[576,128]{1,0:T(8,128)S(1)} %table.1.table_ref, bf16[32768,128]{1,0:T(8,128)(2,1)S(1)} %get-tuple-element.20.psi_ref), custom_call_target="tpu_custom_call" | custom-call | tf_op jit(solution)/shard_map/forward/pallas_call | solution.py:367
  46.7 1.4 %forward.5 = bf16[16,4096]{1,0:T(8,128)(2,1)S(1)} custom-call(s32[132]{0:T(256)S(1)} %get-tuple-element.17.edge_ref, s32[1,32768]{1,0:T(1,128)S(1)} %get-tuple-element.18.seg_ref, f32[576,128]{1,0:T(8,128)S(1)} %table.1.table_ref, bf16[32768,128]{1,0:T(8,128)(2,1)S(1)} %get-tuple-element.20.psi_ref), custom_call_target="tpu_custom_call" | custom-call | tf_op jit(solution)/shard_map/forward/pallas_call | solution.py:367
  48.2 2.8 %collective-permute-start = (bf16[16,4096]{1,0:T(8,128)(2,1)S(1)}, bf16[16,4096]{1,0:T(8,128)(2,1)S(1)}, u32[]{:S(2)}, u32[]{:S(2)}) collective-permute-start(bf16[16,4096]{1,0:T(8,128)(2,1)S(1)} %forward.5), channel_id=1, source_target_pairs={{0,64},{32,96},{64,0},{96,32},{1,65},{33,97},{65,1},{97,33},{2,66}... | collective-permute-start | bytes 393224 | tf_op jit(solution)/shard_map/ppermute | solution.py:356
  51.0 0.3 collective-permute-start.1
  51.3 2.4 %collective-permute-start.2 = (bf16[16,4096]{1,0:T(8,128)(2,1)S(1)}, bf16[16,4096]{1,0:T(8,128)(2,1)S(1)}, u32[]{:S(2)}, u32[]{:S(2)}) collective-permute-start(bf16[16,4096]{1,0:T(8,128)(2,1)S(1)} %forward.7), channel_id=1, source_target_pairs={{0,96},{32,0},{64,32},{96,64},{1,97},{33,1},{65,33},{97,65},{2,98}... | collective-permute-start | bytes 393224 | tf_op jit(solution)/shard_map/ppermute | solution.py:356
  53.7 1.4 %forward.4.a_ref = bf16[16,4096]{1,0:T(8,128)(2,1)S(1)} custom-call(s32[132]{0:T(256)S(1)} %get-tuple-element.17.edge_ref, s32[1,32768]{1,0:T(1,128)S(1)} %get-tuple-element.18.seg_ref, f32[576,128]{1,0:T(8,128)S(1)} %table.1.table_ref, bf16[32768,128]{1,0:T(8,128)(2,1)S(1)} %get-tuple-element.20.psi_ref), custom_call_target="tpu_custom_call" | custom-call | tf_op jit(solution)/shard_map/forward/pallas_call | solution.py:367
  55.1 2.6 %collective-permute-done.1.c_ref = bf16[16,4096]{1,0:T(8,128)(2,1)S(1)} collective-permute-done((bf16[16,4096]{1,0:T(8,128)(2,1)S(1)}, bf16[16,4096]{1,0:T(8,128)(2,1)S(1)}, u32[]{:S(2)}, u32[]{:S(2)}) %collective-permute-start.1) | collective-permute-done | bytes 131104 | tf_op jit(solution)/shard_map/ppermute | solution.py:356
  57.8 2.3 %collective-permute-start.5 = (bf16[16,4096]{1,0:T(8,128)(2,1)S(1)}, bf16[16,4096]{1,0:T(8,128)(2,1)S(1)}, u32[]{:S(2)}, u32[]{:S(2)}) collective-permute-start(bf16[16,4096]{1,0:T(8,128)(2,1)S(1)} %weight.1.w0_ref), channel_id=1, source_target_pairs={{0,96},{32,0},{64,32},{96,64},{1,97},{33,1},{65,33},{97,65},{2,98}... | collective-permute-start | bytes 393224 | tf_op jit(solution)/shard_map/ppermute | solution.py:356
  60.1 1.1 %collective-permute-start.4 = (bf16[16,4096]{1,0:T(8,128)(2,1)S(1)}, bf16[16,4096]{1,0:T(8,128)(2,1)S(1)}, u32[]{:S(2)}, u32[]{:S(2)}) collective-permute-start(bf16[16,4096]{1,0:T(8,128)(2,1)S(1)} %weight.1.w0_ref), channel_id=1, source_target_pairs={{0,64},{32,96},{64,0},{96,32},{1,65},{33,97},{65,1},{97,33},{2,66}... | collective-permute-start | bytes 393224 | tf_op jit(solution)/shard_map/ppermute | solution.py:356
  61.2 1.1 %backward0.1.begun_ref = f32[576,128]{1,0:T(8,128)S(1)} custom-call(s32[132]{0:T(256)S(1)} %get-tuple-element.17.edge_ref, bf16[16,4096]{1,0:T(8,128)(2,1)S(1)} %weight.1.w0_ref, s32[1,32768]{1,0:T(1,128)S(1)} %get-tuple-element.18.seg_ref, bf16[32768,128]{1,0:T(8,128)(2,1)S(1)} %get-tuple-element.20.psi_ref), custom_call_target="tpu_custom_call" | custom-call | tf_op jit(solution)/shard_map/backward0/pallas_call | solution.py:367
  62.2 0.9 collective-permute-done.5.w3_ref
  63.2 2.3 %collective-permute-done.4.w2_ref = bf16[16,4096]{1,0:T(8,128)(2,1)S(1)} collective-permute-done((bf16[16,4096]{1,0:T(8,128)(2,1)S(1)}, bf16[16,4096]{1,0:T(8,128)(2,1)S(1)}, u32[]{:S(2)}, u32[]{:S(2)}) %collective-permute-start.4) | collective-permute-done | bytes 131104 | tf_op jit(solution)/shard_map/ppermute | solution.py:356
  65.5 3.5 %collective-permute-done.3.w1_ref = bf16[16,4096]{1,0:T(8,128)(2,1)S(1)} collective-permute-done((bf16[16,4096]{1,0:T(8,128)(2,1)S(1)}, bf16[16,4096]{1,0:T(8,128)(2,1)S(1)}, u32[]{:S(2)}, u32[]{:S(2)}) %collective-permute-start.3) | collective-permute-done | bytes 131104 | tf_op jit(solution)/shard_map/ppermute | solution.py:356
  69.0 2.2 %backward.1 = bf16[512,128]{1,0:T(8,128)(2,1)S(1)} custom-call(s32[132]{0:T(256)S(1)} %get-tuple-element.17.edge_ref, bf16[16,4096]{1,0:T(8,128)(2,1)S(1)} %collective-permute-done.3.w1_ref, bf16[16,4096]{1,0:T(8,128)(2,1)S(1)} %collective-permute-done.4.w2_ref, bf16[16,4096]{1,0:T(8,128)(2,1)S(1)} %collective-permute-done.5.w3_ref, ...), custom_call_target="tpu_custom_call" | custom-call | tf_op jit(solution)/shard_map/backward/pallas_call | solution.py:367
  71.3 12.1 %all_to_all.22 = bf16[32,16,128]{2,1,0:T(8,128)(2,1)S(1)} all-to-all(bf16[32,16,128]{2,1,0:T(8,128)(2,1)S(1)} %bitcast.18), channel_id=1, replica_groups=mesh['wave'=4,'event'=32] {'event'}, dimensions={0} | all-to-all | bytes 262144 | tf_op jit(solution)/shard_map/all_to_all | solution.py:351
  83.3 7.2 %pull.1 = f32[512,128]{1,0:T(8,128)S(1)} custom-call(bf16[512,128]{1,0:T(8,128)(2,1)S(1)} %bitcast.19, f32[8,2048]{1,0:T(8,128)S(1)} %get-tuple-element.22.scale_ref, bf16[36,4,256,256]{3,2,1,0:T(8,128)(2,1)S(1)} %get-tuple-element.23.kern_ref), custom_call_target="tpu_custom_call" | custom-call | tf_op jit(solution)/shard_map/pull/pallas_call | solution.py:367
  90.5 12.5 %all_to_all.23 = f32[32,16,128]{2,1,0:T(8,128)S(1)} all-to-all(f32[32,16,128]{2,1,0:T(8,128)S(1)} %bitcast.15), channel_id=1, replica_groups=mesh['wave'=4,'event'=32] {'event'}, dimensions={0} | all-to-all | bytes 524288 | tf_op jit(solution)/shard_map/all_to_all | solution.py:351
  103.1 0.8 unpack.1
  (4 shorter events, 0.1 us)
Async XLA Ops:
  48.2 6.9 %collective-permute-start = (bf16[16,4096]{1,0:T(8,128)(2,1)S(1)}, bf16[16,4096]{1,0:T(8,128)(2,1)S(1)}, u32[]{:S(2)}, u32[]{:S(2)}) collective-permute-start(bf16[16,4096]{1,0:T(8,128)(2,1)S(1)} %forward.5), channel_id=1, source_target_pairs={{0,64},{32,96},{64,0},{96,32},{1,65},{33,97},{65,1},{97,33},{2,66}... | collective-permute-start | bytes 393224 | tf_op jit(solution)/shard_map/ppermute | solution.py:356
  51.0 6.7 %collective-permute-start.1 = (bf16[16,4096]{1,0:T(8,128)(2,1)S(1)}, bf16[16,4096]{1,0:T(8,128)(2,1)S(1)}, u32[]{:S(2)}, u32[]{:S(2)}) collective-permute-start(bf16[16,4096]{1,0:T(8,128)(2,1)S(1)} %forward.6), channel_id=1, source_target_pairs={{0,32},{32,64},{64,96},{96,0},{1,33},{33,65},{65,97},{97,1},{2,34}... | collective-permute-start | bytes 393224 | tf_op jit(solution)/shard_map/ppermute | solution.py:356
  51.3 6.4 %collective-permute-start.2 = (bf16[16,4096]{1,0:T(8,128)(2,1)S(1)}, bf16[16,4096]{1,0:T(8,128)(2,1)S(1)}, u32[]{:S(2)}, u32[]{:S(2)}) collective-permute-start(bf16[16,4096]{1,0:T(8,128)(2,1)S(1)} %forward.7), channel_id=1, source_target_pairs={{0,96},{32,0},{64,32},{96,64},{1,97},{33,1},{65,33},{97,65},{2,98}... | collective-permute-start | bytes 393224 | tf_op jit(solution)/shard_map/ppermute | solution.py:356
  57.8 5.3 %collective-permute-start.5 = (bf16[16,4096]{1,0:T(8,128)(2,1)S(1)}, bf16[16,4096]{1,0:T(8,128)(2,1)S(1)}, u32[]{:S(2)}, u32[]{:S(2)}) collective-permute-start(bf16[16,4096]{1,0:T(8,128)(2,1)S(1)} %weight.1.w0_ref), channel_id=1, source_target_pairs={{0,96},{32,0},{64,32},{96,64},{1,97},{33,1},{65,33},{97,65},{2,98}... | collective-permute-start | bytes 393224 | tf_op jit(solution)/shard_map/ppermute | solution.py:356
  60.1 5.4 %collective-permute-start.4 = (bf16[16,4096]{1,0:T(8,128)(2,1)S(1)}, bf16[16,4096]{1,0:T(8,128)(2,1)S(1)}, u32[]{:S(2)}, u32[]{:S(2)}) collective-permute-start(bf16[16,4096]{1,0:T(8,128)(2,1)S(1)} %weight.1.w0_ref), channel_id=1, source_target_pairs={{0,64},{32,96},{64,0},{96,32},{1,65},{33,97},{65,1},{97,33},{2,66}... | collective-permute-start | bytes 393224 | tf_op jit(solution)/shard_map/ppermute | solution.py:356
  61.1 7.9 %collective-permute-start.3 = (bf16[16,4096]{1,0:T(8,128)(2,1)S(1)}, bf16[16,4096]{1,0:T(8,128)(2,1)S(1)}, u32[]{:S(2)}, u32[]{:S(2)}) collective-permute-start(bf16[16,4096]{1,0:T(8,128)(2,1)S(1)} %weight.1.w0_ref), channel_id=1, source_target_pairs={{0,32},{32,64},{64,96},{96,0},{1,33},{33,65},{65,97},{97,1},{2,34}... | collective-permute-start | bytes 393224 | tf_op jit(solution)/shard_map/ppermute | solution.py:356

commit v4 on v3

--- a/solution.py
+++ b/solution.py
@@ -20,6 +20,7 @@
 IN_ROWS = 24
 T = 512
 TILES = E // T
+COST = 10**9
 Q = E // NX
 HQ = Q // 2
 NWIN = 8
@@ -110,7 +111,7 @@
 def gen_kernel(
     r_ref, xy_ref, basis_hbm, bins_hbm, norm_hbm,
     kern_ref, amp_ref, scale_ref, psi_ref, seg_ref, norm_ref, edge_ref,
-    rows_ref, la, x_ref, y_ref, sq_row, sq_col, xy_row, xy_col, dist, bins_ref, sems,
+    rows_ref, la, x_ref, y_ref, sq_row, sq_col, xy_row, xy_col, bins_ref, sems,
 ):
     copies = [
         pltpu.make_async_copy(source, target, sems.at[n])
@@ -160,22 +161,24 @@
             rows = pl.ds(row0 + st * step, step)
             xc = xy_col[0, rows, :].reshape(step // 8, 8, 128)
             yc = xy_col[1, rows, :].reshape(step // 8, 8, 128)
+            near = []
             for c in range(2):
                 half = slice(c * 128, c * 128 + 128)
                 dx = xc - xy_row[0, j, :, half][None]
                 dy = yc - xy_row[1, j, :, half][None]
-                d = -(dx * dx) - dy * dy
-                dist[st * step : st * step + step, half] = d.reshape(step, 128)
-        for q in range(NW):
-            for st in range(TB // step):
-                sq = sq_col[q, pl.ds(row0 + st * step, step), :].reshape(step // 8, 8, 128)
+                near.append(-(dx * dx) - dy * dy)
+            made = range(2) if both or 2 * st * step < TB else range(1, 2)
+            for q in range(NW):
+                sq = sq_col[q, rows, :].reshape(step // 8, 8, 128)
                 parts = []
-                for c in range(2):
-                    half = slice(c * 128, c * 128 + 128)
-                    root = lax.rsqrt(sq + sq_row[q, j, :, half][None])
-                    d = dist[st * step : st * step + step, half].reshape(step // 8, 8, 128)
-                    parts.append((root * jnp.exp2(root * root * d)).reshape(step, 128).astype(BF16))
-                kern_ref[t, q, st * step : st * step + step, :] = jnp.concatenate(parts, axis=1)
+                for c in made:
+                    root = lax.rsqrt(sq + sq_row[q, j, :, c * 128 : c * 128 + 128][None])
+                    parts.append((root * jnp.exp2(root * root * near[c])).reshape(step, 128).astype(BF16))
+                kern_ref[t, q, st * step : st * step + step, made[0] * 128 :] = jnp.concatenate(parts, axis=1)
+        if not both:
+            for q in range(NW):
+                kern_ref[t, q, 128:, 0:128] = kern_ref[t, q, 0:128, 128:].T
+        for q in range(NW):
             times_tile(x_ref, y_ref, q, i, j, kern_ref[t, q], both)
 
     @pl.loop(0, NB, unroll=8)
@@ -217,7 +220,7 @@
     def _(t):
         tile(t, False)
 
-    @pl.loop(NB, NT, unroll=7)
+    @pl.loop(NB, NT, unroll=28)
     def _(t):
         tile(t, True)
 
@@ -319,15 +322,19 @@
                     add(m, half, tile, edge_ref[tile] + w * NWIN)
 
 
-def backward_first_kernel(edge_ref, w0_ref, seg_ref, psi_ref, sums_ref):
+def backward_first_kernel(edge_ref, w_ref, seg_ref, psi_ref, sums_ref):
     sums_ref[...] = jnp.zeros_like(sums_ref)
-    add_quarter(0, edge_ref, w0_ref, seg_ref, psi_ref, sums_ref)
-
-
-def backward_kernel(edge_ref, w1_ref, w2_ref, w3_ref, seg_ref, psi_ref, begun_ref, amp_ref, norm_ref, out_ref, rows_ref, sums):
+    add_quarter(0, edge_ref, w_ref, seg_ref, psi_ref, sums_ref)
+
+
+def backward_next_kernel(k, begun_ref, edge_ref, w_ref, seg_ref, psi_ref, sums_ref):
+    sums_ref[...] = begun_ref[...]
+    add_quarter(k, edge_ref, w_ref, seg_ref, psi_ref, sums_ref)
+
+
+def backward_last_kernel(k, begun_ref, edge_ref, w_ref, seg_ref, psi_ref, amp_ref, norm_ref, out_ref, sums, rows_ref):
     sums[...] = begun_ref[...]
-    for k, w_ref in enumerate((w1_ref, w2_ref, w3_ref)):
-        add_quarter(k + 1, edge_ref, w_ref, seg_ref, psi_ref, sums)
+    add_quarter(k, edge_ref, w_ref, seg_ref, psi_ref, sums)
     rows_ref[...] = amp_ref[...].astype(F32)
     norm = (jnp.concatenate([norm_ref[...]] * 2, axis=0) * (2.0 / S)).T
     for sp in range(SP):
@@ -360,7 +367,7 @@
     return pltpu.VMEM(shape, dtype)
 
 
-def call(kernel, name, out_shape, args, scratch=(), spaces=None, out_specs=None, mib=8):
+def call(kernel, name, out_shape, args, scratch=(), spaces=None, out_specs=None, mib=8, flops=None):
     spaces = spaces or "v" * len(args)
     kept = {"v": pltpu.VMEM, "h": pltpu.HBM}
     args = [pltpu.with_memory_space_constraint(a, kept[c]) if c in kept else a for a, c in zip(args, spaces)]
@@ -371,6 +378,7 @@
         out_specs=out_specs or jax.tree.map(lambda _: VMEM, out_shape),
         scratch_shapes=scratch,
         compiler_params=pltpu.CompilerParams(vmem_limit_bytes=mib * 1024 * 1024),
+        cost_estimate=flops and pl.CostEstimate(flops=flops, bytes_accessed=1 << 20, transcendentals=0),
         name=name,
     )(*args)
 
@@ -412,7 +420,6 @@
             vmem((NW, B, 128), F32),
             vmem((2, NB, 8, TB), F32),
             vmem((2, B, 128), F32),
-            vmem((TB, TB), F32),
             pltpu.SMEM((1, E), jnp.int32),
             pltpu.SemaphoreType.DMA((4,)),
         ],
@@ -426,22 +433,31 @@
 
     def forward(k):
         return call(
-            functools.partial(forward_kernel, k), "forward", vmem((2 * S, HQ)), (edges, seg, table, psi), spaces="svvv"
+            functools.partial(forward_kernel, k), "forward", vmem((2 * S, HQ)), (edges, seg, table, psi), spaces="svvv", flops=COST
         )
 
     others = [shift(forward(k), k) for k in (2, 1, 3)]
     weight = call(weight_kernel, "weight", vmem((2 * S, HQ)), (forward(0), *others))
-    weights = [shift(weight, k) for k in range(1, NX)]
-    begun = call(
-        backward_first_kernel, "backward0", vmem((bins, WL), F32), (edges, weight, seg, psi), spaces="svvv"
-    )
+    sums = call(
+        backward_first_kernel, "backward0", vmem((bins, WL), F32), (edges, weight, seg, psi), spaces="svvv", flops=COST
+    )
+    for k in (3, 1):
+        sums = call(
+            functools.partial(backward_next_kernel, k),
+            "backward1",
+            vmem((bins, WL), F32),
+            (sums, edges, shift(weight, k), seg, psi),
+            spaces="vsvvv",
+            flops=COST,
+        )
     grad_out = call(
-        backward_kernel,
+        functools.partial(backward_last_kernel, 2),
         "backward",
         vmem((G * 16, 128)),
-        (edges, *weights, seg, psi, begun, amp_in, norm),
-        [vmem((G * 16, 128), F32), vmem((bins, WL), F32)],
-        "svvvvvvvv",
+        (sums, edges, shift(weight, 2), seg, psi, amp_in, norm),
+        [vmem((bins, WL), F32), vmem((G * 16, 128), F32)],
+        "vsvvvvv",
+        flops=COST,
     )
     pulled = call(
         pull_kernel,

time: 104 us -> 103 us (level)
  waiting for transfers between devices: 9.42 us -> 6.62 us
  blocking collectives: 53.5 us -> 55.7 us
  starting transfers between devices: 8.81 us -> 7.66 us
    ppermute x6, waiting for transfers between devices: 9.42 us -> 6.62 us  [shift(): return lax.ppermute(x, 'wave', [(i, (i + k) % NX) for i in range(NX)])]
    all_to_all x4, blocking collectives: 53.5 us -> 55.7 us  [exchange(): y = lax.all_to_all(x.reshape(G, rows, 128), 'event', 0, 0)]
    ppermute x6, starting transfers between devices: 8.81 us -> 7.66 us  [shift(): return lax.ppermute(x, 'wave', [(i, (i + k) % NX) for i in range(NX)])]
    pallas_call x12 -> x14, Pallas kernels: 32.1 us -> 32.5 us  [call(): pl.pallas_call(kernel, out_shape=out_shape, in_specs=[{'v': VMEM, 'h': AN...]
  transfers between devices with their start and end apart: 6 -> 6, of which waited for: 4 -> 4; matrix products, arithmetic and copies ran while one was open for 0% -> 0% of each run, Pallas kernels for 2% -> 4%
where the time goes in v4:
time: 103 us
  blocking collectives  55.7 us (54%)
  Pallas kernels  32.5 us (32%)
  starting transfers between devices  7.66 us (7%)
  waiting for transfers between devices  6.62 us (6%)
    all_to_all x4, blocking collectives, exchange(): y = lax.all_to_all(x.reshape(G, rows, 128), 'event', 0, 0)  55.7 us
    pallas_call x14, Pallas kernels, call(): pl.pallas_call(kernel, out_shape=out_shape, in_specs=[{'v': VMEM, 'h': AN...  32.5 us
    ppermute x6, starting transfers between devices, shift(): return lax.ppermute(x, 'wave', [(i, (i + k) % NX) for i in range(NX)])  7.66 us
    ppermute x6, waiting for transfers between devices, shift(): return lax.ppermute(x, 'wave', [(i, (i + k) % NX) for i in range(NX)])  6.62 us
  transfers between devices with their start and end apart: 6, of which 4 were waited for; matrix products, arithmetic and copies ran while one was open for 0% of the time, Pallas kernels for 4%

profile of v4, /device:TPU:1, one launch (start us, length us, event | category | flops | bytes accessed | tf_op | source)
XLA Modules:
  0.0 102.5 jit_solution(11058322185543986496)
XLA Ops:
  0.0 1.2 %pack.1 = (bf16[768,128]{1,0:T(8,128)(2,1)S(1)}, f32[2,2048]{1,0:T(2,128)S(1)}, bf16[8,64,128]{2,1,0:T(8,128)(2,1)S(1)}) custom-call(bf16[8,64,128]{2,1,0:T(8,128)(2,1)} %bitcast.22, f32[64,128]{1,0:T(8,128)} %bitcast.24, f32[64,128]{1,0:T(8,128)} %bitcast.25, f32[2,2048]{1,0:T(2,128)} %xy_hbm.1), custom_call_target="tpu_custom_call" | custom-call | tf_op jit(solution)/shard_map/pack/pallas_call | solution.py:374
  1.2 17.7 %all_to_all.20 = bf16[32,24,128]{2,1,0:T(8,128)(2,1)S(1)} all-to-all(bf16[32,24,128]{2,1,0:T(8,128)(2,1)S(1)} %bitcast.20), channel_id=1, replica_groups=mesh['wave'=4,'event'=32] {'event'}, dimensions={0} | all-to-all | bytes 393216 | tf_op jit(solution)/shard_map/all_to_all | solution.py:358
  18.8 13.5 %gen.1 = (bf16[36,4,256,256]{3,2,1,0:T(8,128)(2,1)S(1)}, bf16[512,128]{1,0:T(8,128)(2,1)S(1)}, f32[8,2048]{1,0:T(8,128)S(1)}, bf16[32768,128]{1,0:T(8,128)(2,1)S...) custom-call(bf16[768,128]{1,0:T(8,128)(2,1)S(1)} %bitcast.17, ...), custom_call_target="tpu_custom_call" | custom-call | tf_op jit(solution)/shard_map/gen/pallas_call | solution.py:374
  32.3 11.2 %all_to_all.21 = bf16[32,16,128]{2,1,0:T(8,128)(2,1)S(1)} all-to-all(bf16[32,16,128]{2,1,0:T(8,128)(2,1)S(1)} %bitcast.21), channel_id=1, replica_groups=mesh['wave'=4,'event'=32] {'event'}, dimensions={0} | all-to-all | bytes 262144 | tf_op jit(solution)/shard_map/all_to_all | solution.py:358
  43.7 1.4 %forward.7 = bf16[16,4096]{1,0:T(8,128)(2,1)S(1)} custom-call(s32[132]{0:T(256)S(1)} %get-tuple-element.17.edge_ref, s32[1,32768]{1,0:T(1,128)S(1)} %get-tuple-element.18.seg_ref, f32[576,128]{1,0:T(8,128)S(1)} %table.1.table_ref, bf16[32768,128]{1,0:T(8,128)(2,1)S(1)} %get-tuple-element.20.psi_ref), custom_call_target="tpu_custom_call" | custom-call | flops 1000000000 | bytes 1048576 | tf_op jit(solution)/shard_map/forward/pallas_call | solution.py:374
  45.2 1.4 %forward.6 = bf16[16,4096]{1,0:T(8,128)(2,1)S(1)} custom-call(s32[132]{0:T(256)S(1)} %get-tuple-element.17.edge_ref, s32[1,32768]{1,0:T(1,128)S(1)} %get-tuple-element.18.seg_ref, f32[576,128]{1,0:T(8,128)S(1)} %table.1.table_ref, bf16[32768,128]{1,0:T(8,128)(2,1)S(1)} %get-tuple-element.20.psi_ref), custom_call_target="tpu_custom_call" | custom-call | flops 1000000000 | bytes 1048576 | tf_op jit(solution)/shard_map/forward/pallas_call | solution.py:374
  46.6 1.4 %forward.5 = bf16[16,4096]{1,0:T(8,128)(2,1)S(1)} custom-call(s32[132]{0:T(256)S(1)} %get-tuple-element.17.edge_ref, s32[1,32768]{1,0:T(1,128)S(1)} %get-tuple-element.18.seg_ref, f32[576,128]{1,0:T(8,128)S(1)} %table.1.table_ref, bf16[32768,128]{1,0:T(8,128)(2,1)S(1)} %get-tuple-element.20.psi_ref), custom_call_target="tpu_custom_call" | custom-call | flops 1000000000 | bytes 1048576 | tf_op jit(solution)/shard_map/forward/pallas_call | solution.py:374
  48.0 2.5 %collective-permute-start.2 = (bf16[16,4096]{1,0:T(8,128)(2,1)S(1)}, bf16[16,4096]{1,0:T(8,128)(2,1)S(1)}, u32[]{:S(2)}, u32[]{:S(2)}) collective-permute-start(bf16[16,4096]{1,0:T(8,128)(2,1)S(1)} %forward.7), channel_id=1, source_target_pairs={{0,96},{32,0},{64,32},{96,64},{1,97},{33,1},{65,33},{97,65},{2,98}... | collective-permute-start | bytes 393224 | tf_op jit(solution)/shard_map/ppermute | solution.py:363
  50.5 1.7 %collective-permute-start = (bf16[16,4096]{1,0:T(8,128)(2,1)S(1)}, bf16[16,4096]{1,0:T(8,128)(2,1)S(1)}, u32[]{:S(2)}, u32[]{:S(2)}) collective-permute-start(bf16[16,4096]{1,0:T(8,128)(2,1)S(1)} %forward.5), channel_id=1, source_target_pairs={{0,64},{32,96},{64,0},{96,32},{1,65},{33,97},{65,1},{97,33},{2,66}... | collective-permute-start | bytes 393224 | tf_op jit(solution)/shard_map/ppermute | solution.py:363
  52.3 1.4 %forward.4.a_ref = bf16[16,4096]{1,0:T(8,128)(2,1)S(1)} custom-call(s32[132]{0:T(256)S(1)} %get-tuple-element.17.edge_ref, s32[1,32768]{1,0:T(1,128)S(1)} %get-tuple-element.18.seg_ref, f32[576,128]{1,0:T(8,128)S(1)} %table.1.table_ref, bf16[32768,128]{1,0:T(8,128)(2,1)S(1)} %get-tuple-element.20.psi_ref), custom_call_target="tpu_custom_call" | custom-call | flops 1000000000 | bytes 1048576 | tf_op jit(solution)/shard_map/forward/pallas_call | solution.py:374
  53.7 3.9 %collective-permute-done.1.c_ref = bf16[16,4096]{1,0:T(8,128)(2,1)S(1)} collective-permute-done((bf16[16,4096]{1,0:T(8,128)(2,1)S(1)}, bf16[16,4096]{1,0:T(8,128)(2,1)S(1)}, u32[]{:S(2)}, u32[]{:S(2)}) %collective-permute-start.1) | collective-permute-done | bytes 131104 | tf_op jit(solution)/shard_map/ppermute | solution.py:363
  57.5 0.4 collective-permute-done.b_ref
  58.1 0.7 collective-permute-start.3
  58.7 0.9 collective-permute-start.4
  59.6 1.1 %backward0.1.begun_ref = f32[576,128]{1,0:T(8,128)S(1)} custom-call(s32[132]{0:T(256)S(1)} %get-tuple-element.17.edge_ref, bf16[16,4096]{1,0:T(8,128)(2,1)S(1)} %weight.1.w_ref, s32[1,32768]{1,0:T(1,128)S(1)} %get-tuple-element.18.seg_ref, bf16[32768,128]{1,0:T(8,128)(2,1)S(1)} %get-tuple-element.20.psi_ref), custom_call_target="tpu_custom_call" | custom-call | flops 1000000000 | bytes 1048576 | tf_op jit(solution)/shard_map/backward0/pallas_call | solution.py:374
  60.7 1.9 %collective-permute-start.5 = (bf16[16,4096]{1,0:T(8,128)(2,1)S(1)}, bf16[16,4096]{1,0:T(8,128)(2,1)S(1)}, u32[]{:S(2)}, u32[]{:S(2)}) collective-permute-start(bf16[16,4096]{1,0:T(8,128)(2,1)S(1)} %weight.1.w_ref), channel_id=1, source_target_pairs={{0,64},{32,96},{64,0},{96,32},{1,65},{33,97},{65,1},{97,33},{2,66}... | collective-permute-start | bytes 393224 | tf_op jit(solution)/shard_map/ppermute | solution.py:363
  62.5 1.1 %backward1.2.begun_ref = f32[576,128]{1,0:T(8,128)S(1)} custom-call(f32[576,128]{1,0:T(8,128)S(1)} %backward0.1.begun_ref, s32[132]{0:T(256)S(1)} %get-tuple-element.17.edge_ref, bf16[16,4096]{1,0:T(8,128)(2,1)S(1)} %collective-permute-done.3.w_ref, s32[1,32768]{1,0:T(1,128)S(1)} %get-tuple-element.18.seg_ref, bf16[32768,128]{1,0:T(8,128)(2,1)S(1)} %get-tuple-element.20.psi_ref), custom_call_target="tpu_custom_call" | custom-call | flops 1000000000 | bytes 1048576 | tf_op jit(solution)/shard_map/backward1/pallas_call | solution.py:374
  63.8 1.1 %backward1.3.begun_ref = f32[576,128]{1,0:T(8,128)S(1)} custom-call(f32[576,128]{1,0:T(8,128)S(1)} %backward1.2.begun_ref, s32[132]{0:T(256)S(1)} %get-tuple-element.17.edge_ref, bf16[16,4096]{1,0:T(8,128)(2,1)S(1)} %collective-permute-done.4.w_ref, s32[1,32768]{1,0:T(1,128)S(1)} %get-tuple-element.18.seg_ref, bf16[32768,128]{1,0:T(8,128)(2,1)S(1)} %get-tuple-element.20.psi_ref), custom_call_target="tpu_custom_call" | custom-call | flops 1000000000 | bytes 1048576 | tf_op jit(solution)/shard_map/backward1/pallas_call | solution.py:374
  64.8 2.2 %collective-permute-done.5.w_ref = bf16[16,4096]{1,0:T(8,128)(2,1)S(1)} collective-permute-done((bf16[16,4096]{1,0:T(8,128)(2,1)S(1)}, bf16[16,4096]{1,0:T(8,128)(2,1)S(1)}, u32[]{:S(2)}, u32[]{:S(2)}) %collective-permute-start.5) | collective-permute-done | bytes 131104 | tf_op jit(solution)/shard_map/ppermute | solution.py:363
  67.0 1.3 %backward.1 = bf16[512,128]{1,0:T(8,128)(2,1)S(1)} custom-call(f32[576,128]{1,0:T(8,128)S(1)} %backward1.3.begun_ref, s32[132]{0:T(256)S(1)} %get-tuple-element.17.edge_ref, bf16[16,4096]{1,0:T(8,128)(2,1)S(1)} %collective-permute-done.5.w_ref, s32[1,32768]{1,0:T(1,128)S(1)} %get-tuple-element.18.seg_ref, bf16[32768,128]{1,0:T(8,128)(2,1)S(1)} %get-tuple-element.20.psi_ref, ...), custom_call_target="tpu_custom_call" | custom-call | flops 1000000000 | bytes 1048576 | tf_op jit(solution)/shard_map/backward/pallas_call | solution.py:374
  68.3 14.2 %all_to_all.22 = bf16[32,16,128]{2,1,0:T(8,128)(2,1)S(1)} all-to-all(bf16[32,16,128]{2,1,0:T(8,128)(2,1)S(1)} %bitcast.18), channel_id=1, replica_groups=mesh['wave'=4,'event'=32] {'event'}, dimensions={0} | all-to-all | bytes 262144 | tf_op jit(solution)/shard_map/all_to_all | solution.py:358
  82.5 6.6 %pull.1 = f32[512,128]{1,0:T(8,128)S(1)} custom-call(bf16[512,128]{1,0:T(8,128)(2,1)S(1)} %bitcast.19, f32[8,2048]{1,0:T(8,128)S(1)} %get-tuple-element.22.scale_ref, bf16[36,4,256,256]{3,2,1,0:T(8,128)(2,1)S(1)} %get-tuple-element.23.kern_ref), custom_call_target="tpu_custom_call" | custom-call | tf_op jit(solution)/shard_map/pull/pallas_call | solution.py:374
  89.1 12.6 %all_to_all.23 = f32[32,16,128]{2,1,0:T(8,128)S(1)} all-to-all(f32[32,16,128]{2,1,0:T(8,128)S(1)} %bitcast.15), channel_id=1, replica_groups=mesh['wave'=4,'event'=32] {'event'}, dimensions={0} | all-to-all | bytes 524288 | tf_op jit(solution)/shard_map/all_to_all | solution.py:358
  101.7 0.8 unpack.1
  (6 shorter events, 0.4 us)
Async XLA Ops:
  48.0 5.7 %collective-permute-start.2 = (bf16[16,4096]{1,0:T(8,128)(2,1)S(1)}, bf16[16,4096]{1,0:T(8,128)(2,1)S(1)}, u32[]{:S(2)}, u32[]{:S(2)}) collective-permute-start(bf16[16,4096]{1,0:T(8,128)(2,1)S(1)} %forward.7), channel_id=1, source_target_pairs={{0,96},{32,0},{64,32},{96,64},{1,97},{33,1},{65,33},{97,65},{2,98}... | collective-permute-start | bytes 393224 | tf_op jit(solution)/shard_map/ppermute | solution.py:363
  50.5 7.0 %collective-permute-start.1 = (bf16[16,4096]{1,0:T(8,128)(2,1)S(1)}, bf16[16,4096]{1,0:T(8,128)(2,1)S(1)}, u32[]{:S(2)}, u32[]{:S(2)}) collective-permute-start(bf16[16,4096]{1,0:T(8,128)(2,1)S(1)} %forward.6), channel_id=1, source_target_pairs={{0,32},{32,64},{64,96},{96,0},{1,33},{33,65},{65,97},{97,1},{2,34}... | collective-permute-start | bytes 393224 | tf_op jit(solution)/shard_map/ppermute | solution.py:363
  50.5 7.4 %collective-permute-start = (bf16[16,4096]{1,0:T(8,128)(2,1)S(1)}, bf16[16,4096]{1,0:T(8,128)(2,1)S(1)}, u32[]{:S(2)}, u32[]{:S(2)}) collective-permute-start(bf16[16,4096]{1,0:T(8,128)(2,1)S(1)} %forward.5), channel_id=1, source_target_pairs={{0,64},{32,96},{64,0},{96,32},{1,65},{33,97},{65,1},{97,33},{2,66}... | collective-permute-start | bytes 393224 | tf_op jit(solution)/shard_map/ppermute | solution.py:363
  58.1 4.5 %collective-permute-start.3 = (bf16[16,4096]{1,0:T(8,128)(2,1)S(1)}, bf16[16,4096]{1,0:T(8,128)(2,1)S(1)}, u32[]{:S(2)}, u32[]{:S(2)}) collective-permute-start(bf16[16,4096]{1,0:T(8,128)(2,1)S(1)} %weight.1.w_ref), channel_id=1, source_target_pairs={{0,96},{32,0},{64,32},{96,64},{1,97},{33,1},{65,33},{97,65},{2,98}... | collective-permute-start | bytes 393224 | tf_op jit(solution)/shard_map/ppermute | solution.py:363
  58.7 5.0 %collective-permute-start.4 = (bf16[16,4096]{1,0:T(8,128)(2,1)S(1)}, bf16[16,4096]{1,0:T(8,128)(2,1)S(1)}, u32[]{:S(2)}, u32[]{:S(2)}) collective-permute-start(bf16[16,4096]{1,0:T(8,128)(2,1)S(1)} %weight.1.w_ref), channel_id=1, source_target_pairs={{0,32},{32,64},{64,96},{96,0},{1,33},{33,65},{65,97},{97,1},{2,34}... | collective-permute-start | bytes 393224 | tf_op jit(solution)/shard_map/ppermute | solution.py:363
  60.7 6.4 %collective-permute-start.5 = (bf16[16,4096]{1,0:T(8,128)(2,1)S(1)}, bf16[16,4096]{1,0:T(8,128)(2,1)S(1)}, u32[]{:S(2)}, u32[]{:S(2)}) collective-permute-start(bf16[16,4096]{1,0:T(8,128)(2,1)S(1)} %weight.1.w_ref), channel_id=1, source_target_pairs={{0,64},{32,96},{64,0},{96,32},{1,65},{33,97},{65,1},{97,33},{2,66}... | collective-permute-start | bytes 393224 | tf_op jit(solution)/shard_map/ppermute | solution.py:363

commit v5 on v4

--- a/solution.py
+++ b/solution.py
@@ -78,11 +78,11 @@
 
 
 def times_tile(x_ref, y_ref, q, i, j, tile, both):
-    y_ref[q, j] += jnp.dot(x_ref[q, i], tile, preferred_element_type=F32)
     if both:
         y_ref[q, i] += lax.dot_general(
             x_ref[q, j], tile, (((1,), (1,)), ((), ())), preferred_element_type=F32
         )
+    y_ref[q, j] += jnp.dot(x_ref[q, i], tile, preferred_element_type=F32)
 
 
 def tile_place(t):
@@ -185,7 +185,7 @@
     def _(t):
         tile(t, False)
 
-    @pl.loop(NB, NT, unroll=7)
+    @pl.loop(NB, NT, unroll=14)
     def _(t):
         tile(t, True)
 
@@ -425,7 +425,7 @@
         ],
         "vvhhh",
         (VMEM,) * 6 + (SMEM,),
-        mib=12,
+        mib=20,
     )
     amp_in = exchange(amp_out, 16)
     bins = (R + NWIN) * S

time: 103 us -> 115 us (1.12)
  local copies, waits for them, and re-layouts: 0 us -> 12.8 us
    unnamed x0 -> x4, local copies, waits for them, and re-layouts: none -> 12.8 us
where the time goes in v5:
time: 115 us; the launch traced here: 114 us
  blocking collectives  55.5 us (48%)
  Pallas kernels  31.8 us (28%)
  local copies, waits for them, and re-layouts  12.8 us (11%)
  starting transfers between devices  7.47 us (6%)
  waiting for transfers between devices  6.81 us (6%)
    all_to_all x4, blocking collectives, exchange(): y = lax.all_to_all(x.reshape(G, rows, 128), 'event', 0, 0)  55.5 us
    pallas_call x14, Pallas kernels, call(): pl.pallas_call(kernel, out_shape=out_shape, in_specs=[{'v': VMEM, 'h': AN...  31.8 us
    unnamed x4, local copies, waits for them, and re-layouts  12.8 us
    ppermute x6, starting transfers between devices, shift(): return lax.ppermute(x, 'wave', [(i, (i + k) % NX) for i in range(NX)])  7.47 us
    ppermute x6, waiting for transfers between devices, shift(): return lax.ppermute(x, 'wave', [(i, (i + k) % NX) for i in range(NX)])  6.81 us
  transfers between devices with their start and end apart: 6, of which 4 were waited for; matrix products, arithmetic and copies ran while one was open for 0% of the time, Pallas kernels for 4%

profile of v5, /device:TPU:1, one launch (start us, length us, event | category | flops | bytes accessed | tf_op | source)
XLA Modules:
  0.0 114.4 jit_solution(17949733165992140209)
XLA Ops:
  0.0 1.2 %pack.1 = (bf16[768,128]{1,0:T(8,128)(2,1)S(1)}, f32[2,2048]{1,0:T(2,128)S(1)}, bf16[8,64,128]{2,1,0:T(8,128)(2,1)S(1)}) custom-call(bf16[8,64,128]{2,1,0:T(8,128)(2,1)} %bitcast.22, f32[64,128]{1,0:T(8,128)} %bitcast.24, f32[64,128]{1,0:T(8,128)} %bitcast.25, f32[2,2048]{1,0:T(2,128)} %xy_hbm.1), custom_call_target="tpu_custom_call" | custom-call | tf_op jit(solution)/shard_map/pack/pallas_call | solution.py:374
  1.2 17.7 %all_to_all.20 = bf16[32,24,128]{2,1,0:T(8,128)(2,1)S(1)} all-to-all(bf16[32,24,128]{2,1,0:T(8,128)(2,1)S(1)} %bitcast.20), channel_id=1, replica_groups=mesh['wave'=4,'event'=32] {'event'}, dimensions={0} | all-to-all | bytes 393216 | tf_op jit(solution)/shard_map/all_to_all | solution.py:358
  18.8 12.8 %gen.1 = (bf16[36,4,256,256]{3,2,1,0:T(8,128)(2,1)S(1)}, bf16[512,128]{1,0:T(8,128)(2,1)S(1)}, f32[8,2048]{1,0:T(8,128)S(1)}, bf16[32768,128]{1,0:T(8,128)(2,1)S...) custom-call(bf16[768,128]{1,0:T(8,128)(2,1)S(1)} %bitcast.17, ...), custom_call_target="tpu_custom_call" | custom-call | tf_op jit(solution)/shard_map/gen/pallas_call | solution.py:374
  31.6 6.5 %copy-done = bf16[36,4,256,256]{3,2,1,0:T(8,128)(2,1)} copy-done((bf16[36,4,256,256]{3,2,1,0:T(8,128)(2,1)}, bf16[36,4,256,256]{3,2,1,0:T(8,128)(2,1)S(1)}, u32[]{:S(2)}) %copy-start) | copy-done | bytes 18874392
  38.1 11.2 %all_to_all.21 = bf16[32,16,128]{2,1,0:T(8,128)(2,1)S(1)} all-to-all(bf16[32,16,128]{2,1,0:T(8,128)(2,1)S(1)} %bitcast.21), channel_id=1, replica_groups=mesh['wave'=4,'event'=32] {'event'}, dimensions={0} | all-to-all | bytes 262144 | tf_op jit(solution)/shard_map/all_to_all | solution.py:358
  49.5 1.4 %forward.7 = bf16[16,4096]{1,0:T(8,128)(2,1)S(1)} custom-call(s32[132]{0:T(256)S(1)} %get-tuple-element.17.edge_ref, s32[1,32768]{1,0:T(1,128)S(1)} %get-tuple-element.18.seg_ref, f32[576,128]{1,0:T(8,128)S(1)} %table.1.table_ref, bf16[32768,128]{1,0:T(8,128)(2,1)S(1)} %get-tuple-element.20.psi_ref), custom_call_target="tpu_custom_call" | custom-call | flops 1000000000 | bytes 1048576 | tf_op jit(solution)/shard_map/forward/pallas_call | solution.py:374
  50.9 1.4 %forward.6 = bf16[16,4096]{1,0:T(8,128)(2,1)S(1)} custom-call(s32[132]{0:T(256)S(1)} %get-tuple-element.17.edge_ref, s32[1,32768]{1,0:T(1,128)S(1)} %get-tuple-element.18.seg_ref, f32[576,128]{1,0:T(8,128)S(1)} %table.1.table_ref, bf16[32768,128]{1,0:T(8,128)(2,1)S(1)} %get-tuple-element.20.psi_ref), custom_call_target="tpu_custom_call" | custom-call | flops 1000000000 | bytes 1048576 | tf_op jit(solution)/shard_map/forward/pallas_call | solution.py:374
  52.3 1.4 %forward.5 = bf16[16,4096]{1,0:T(8,128)(2,1)S(1)} custom-call(s32[132]{0:T(256)S(1)} %get-tuple-element.17.edge_ref, s32[1,32768]{1,0:T(1,128)S(1)} %get-tuple-element.18.seg_ref, f32[576,128]{1,0:T(8,128)S(1)} %table.1.table_ref, bf16[32768,128]{1,0:T(8,128)(2,1)S(1)} %get-tuple-element.20.psi_ref), custom_call_target="tpu_custom_call" | custom-call | flops 1000000000 | bytes 1048576 | tf_op jit(solution)/shard_map/forward/pallas_call | solution.py:374
  53.7 2.5 %collective-permute-start.2 = (bf16[16,4096]{1,0:T(8,128)(2,1)S(1)}, bf16[16,4096]{1,0:T(8,128)(2,1)S(1)}, u32[]{:S(2)}, u32[]{:S(2)}) collective-permute-start(bf16[16,4096]{1,0:T(8,128)(2,1)S(1)} %forward.7), channel_id=1, source_target_pairs={{0,96},{32,0},{64,32},{96,64},{1,97},{33,1},{65,33},{97,65},{2,98}... | collective-permute-start | bytes 393224 | tf_op jit(solution)/shard_map/ppermute | solution.py:363
  56.3 1.7 %collective-permute-start = (bf16[16,4096]{1,0:T(8,128)(2,1)S(1)}, bf16[16,4096]{1,0:T(8,128)(2,1)S(1)}, u32[]{:S(2)}, u32[]{:S(2)}) collective-permute-start(bf16[16,4096]{1,0:T(8,128)(2,1)S(1)} %forward.5), channel_id=1, source_target_pairs={{0,64},{32,96},{64,0},{96,32},{1,65},{33,97},{65,1},{97,33},{2,66}... | collective-permute-start | bytes 393224 | tf_op jit(solution)/shard_map/ppermute | solution.py:363
  58.0 1.4 %forward.4.a_ref = bf16[16,4096]{1,0:T(8,128)(2,1)S(1)} custom-call(s32[132]{0:T(256)S(1)} %get-tuple-element.17.edge_ref, s32[1,32768]{1,0:T(1,128)S(1)} %get-tuple-element.18.seg_ref, f32[576,128]{1,0:T(8,128)S(1)} %table.1.table_ref, bf16[32768,128]{1,0:T(8,128)(2,1)S(1)} %get-tuple-element.20.psi_ref), custom_call_target="tpu_custom_call" | custom-call | flops 1000000000 | bytes 1048576 | tf_op jit(solution)/shard_map/forward/pallas_call | solution.py:374
  59.4 3.8 %collective-permute-done.1.c_ref = bf16[16,4096]{1,0:T(8,128)(2,1)S(1)} collective-permute-done((bf16[16,4096]{1,0:T(8,128)(2,1)S(1)}, bf16[16,4096]{1,0:T(8,128)(2,1)S(1)}, u32[]{:S(2)}, u32[]{:S(2)}) %collective-permute-start.1) | collective-permute-done | bytes 131104 | tf_op jit(solution)/shard_map/ppermute | solution.py:363
  64.4 0.9 collective-permute-start.4
  65.3 1.1 backward0.1.begun_ref
  66.4 1.7 %collective-permute-start.5 = (bf16[16,4096]{1,0:T(8,128)(2,1)S(1)}, bf16[16,4096]{1,0:T(8,128)(2,1)S(1)}, u32[]{:S(2)}, u32[]{:S(2)}) collective-permute-start(bf16[16,4096]{1,0:T(8,128)(2,1)S(1)} %weight.1.w_ref), channel_id=1, source_target_pairs={{0,64},{32,96},{64,0},{96,32},{1,65},{33,97},{65,1},{97,33},{2,66}... | collective-permute-start | bytes 393224 | tf_op jit(solution)/shard_map/ppermute | solution.py:363
  68.1 1.1 backward1.2.begun_ref
  69.5 1.1 backward1.3.begun_ref
  70.5 2.2 %collective-permute-done.5.w_ref = bf16[16,4096]{1,0:T(8,128)(2,1)S(1)} collective-permute-done((bf16[16,4096]{1,0:T(8,128)(2,1)S(1)}, bf16[16,4096]{1,0:T(8,128)(2,1)S(1)}, u32[]{:S(2)}, u32[]{:S(2)}) %collective-permute-start.5) | collective-permute-done | bytes 131104 | tf_op jit(solution)/shard_map/ppermute | solution.py:363
  72.7 1.3 %backward.1 = bf16[512,128]{1,0:T(8,128)(2,1)S(1)} custom-call(f32[576,128]{1,0:T(8,128)S(1)} %backward1.3.begun_ref, s32[132]{0:T(256)S(1)} %get-tuple-element.17.edge_ref, bf16[16,4096]{1,0:T(8,128)(2,1)S(1)} %collective-permute-done.5.w_ref, s32[1,32768]{1,0:T(1,128)S(1)} %get-tuple-element.18.seg_ref, bf16[32768,128]{1,0:T(8,128)(2,1)S(1)} %get-tuple-element.20.psi_ref, ...), custom_call_target="tpu_custom_call" | custom-call | flops 1000000000 | bytes 1048576 | tf_op jit(solution)/shard_map/backward/pallas_call | solution.py:374
  74.0 14.0 %all_to_all.22 = bf16[32,16,128]{2,1,0:T(8,128)(2,1)S(1)} all-to-all(bf16[32,16,128]{2,1,0:T(8,128)(2,1)S(1)} %bitcast.18), channel_id=1, replica_groups=mesh['wave'=4,'event'=32] {'event'}, dimensions={0} | all-to-all | bytes 262144 | tf_op jit(solution)/shard_map/all_to_all | solution.py:358
  88.1 6.4 %copy-done.1 = bf16[36,4,256,256]{3,2,1,0:T(8,128)(2,1)S(1)} copy-done((bf16[36,4,256,256]{3,2,1,0:T(8,128)(2,1)S(1)}, bf16[36,4,256,256]{3,2,1,0:T(8,128)(2,1)}, u32[]{:S(2)}) %copy-start.1) | copy-done | bytes 18874392
  94.5 6.6 %pull.1 = f32[512,128]{1,0:T(8,128)S(1)} custom-call(bf16[512,128]{1,0:T(8,128)(2,1)S(1)} %bitcast.19, f32[8,2048]{1,0:T(8,128)S(1)} %get-tuple-element.22.scale_ref, bf16[36,4,256,256]{3,2,1,0:T(8,128)(2,1)S(1)} %copy-done.1), custom_call_target="tpu_custom_call" | custom-call | tf_op jit(solution)/shard_map/pull/pallas_call | solution.py:374
  101.0 12.5 %all_to_all.23 = f32[32,16,128]{2,1,0:T(8,128)S(1)} all-to-all(f32[32,16,128]{2,1,0:T(8,128)S(1)} %bitcast.15), channel_id=1, replica_groups=mesh['wave'=4,'event'=32] {'event'}, dimensions={0} | all-to-all | bytes 524288 | tf_op jit(solution)/shard_map/all_to_all | solution.py:358
  113.6 0.8 unpack.1
  (10 shorter events, 1.7 us)
Async XLA Ops:
  31.6 6.5 %copy-start = (bf16[36,4,256,256]{3,2,1,0:T(8,128)(2,1)}, bf16[36,4,256,256]{3,2,1,0:T(8,128)(2,1)S(1)}, u32[]{:S(2)}) copy-start(bf16[36,4,256,256]{3,2,1,0:T(8,128)(2,1)S(1)} %get-tuple-element.23.kern_ref) | copy-start | bytes 56623108
  53.7 5.7 %collective-permute-start.2 = (bf16[16,4096]{1,0:T(8,128)(2,1)S(1)}, bf16[16,4096]{1,0:T(8,128)(2,1)S(1)}, u32[]{:S(2)}, u32[]{:S(2)}) collective-permute-start(bf16[16,4096]{1,0:T(8,128)(2,1)S(1)} %forward.7), channel_id=1, source_target_pairs={{0,96},{32,0},{64,32},{96,64},{1,97},{33,1},{65,33},{97,65},{2,98}... | collective-permute-start | bytes 393224 | tf_op jit(solution)/shard_map/ppermute | solution.py:363
  56.3 7.0 %collective-permute-start.1 = (bf16[16,4096]{1,0:T(8,128)(2,1)S(1)}, bf16[16,4096]{1,0:T(8,128)(2,1)S(1)}, u32[]{:S(2)}, u32[]{:S(2)}) collective-permute-start(bf16[16,4096]{1,0:T(8,128)(2,1)S(1)} %forward.6), channel_id=1, source_target_pairs={{0,32},{32,64},{64,96},{96,0},{1,33},{33,65},{65,97},{97,1},{2,34}... | collective-permute-start | bytes 393224 | tf_op jit(solution)/shard_map/ppermute | solution.py:363
  56.3 7.4 %collective-permute-start = (bf16[16,4096]{1,0:T(8,128)(2,1)S(1)}, bf16[16,4096]{1,0:T(8,128)(2,1)S(1)}, u32[]{:S(2)}, u32[]{:S(2)}) collective-permute-start(bf16[16,4096]{1,0:T(8,128)(2,1)S(1)} %forward.5), channel_id=1, source_target_pairs={{0,64},{32,96},{64,0},{96,32},{1,65},{33,97},{65,1},{97,33},{2,66}... | collective-permute-start | bytes 393224 | tf_op jit(solution)/shard_map/ppermute | solution.py:363
  63.8 4.3 %collective-permute-start.3 = (bf16[16,4096]{1,0:T(8,128)(2,1)S(1)}, bf16[16,4096]{1,0:T(8,128)(2,1)S(1)}, u32[]{:S(2)}, u32[]{:S(2)}) collective-permute-start(bf16[16,4096]{1,0:T(8,128)(2,1)S(1)} %weight.1.w_ref), channel_id=1, source_target_pairs={{0,96},{32,0},{64,32},{96,64},{1,97},{33,1},{65,33},{97,65},{2,98}... | collective-permute-start | bytes 393224 | tf_op jit(solution)/shard_map/ppermute | solution.py:363
  64.4 5.0 %collective-permute-start.4 = (bf16[16,4096]{1,0:T(8,128)(2,1)S(1)}, bf16[16,4096]{1,0:T(8,128)(2,1)S(1)}, u32[]{:S(2)}, u32[]{:S(2)}) collective-permute-start(bf16[16,4096]{1,0:T(8,128)(2,1)S(1)} %weight.1.w_ref), channel_id=1, source_target_pairs={{0,32},{32,64},{64,96},{96,0},{1,33},{33,65},{65,97},{97,1},{2,34}... | collective-permute-start | bytes 393224 | tf_op jit(solution)/shard_map/ppermute | solution.py:363
  66.4 6.3 %collective-permute-start.5 = (bf16[16,4096]{1,0:T(8,128)(2,1)S(1)}, bf16[16,4096]{1,0:T(8,128)(2,1)S(1)}, u32[]{:S(2)}, u32[]{:S(2)}) collective-permute-start(bf16[16,4096]{1,0:T(8,128)(2,1)S(1)} %weight.1.w_ref), channel_id=1, source_target_pairs={{0,64},{32,96},{64,0},{96,32},{1,65},{33,97},{65,1},{97,33},{2,66}... | collective-permute-start | bytes 393224 | tf_op jit(solution)/shard_map/ppermute | solution.py:363
  88.1 6.4 %copy-start.1 = (bf16[36,4,256,256]{3,2,1,0:T(8,128)(2,1)S(1)}, bf16[36,4,256,256]{3,2,1,0:T(8,128)(2,1)}, u32[]{:S(2)}) copy-start(bf16[36,4,256,256]{3,2,1,0:T(8,128)(2,1)} %copy-done) | copy-start | bytes 56623108
